TPU v7x, 32 devices: a whole 2x2x4 slice. The times are simulated.
32 devices in a mesh: runs: 2 (over y), gx: 4 (over z), gy: 2 (over x), gz: 2 (over core).
Axes of the slice: x: 2, y: 2, z: 4, core: 2. Of those that a mesh axis runs over, the one named last changes fastest.
Arguments:
- row_owner: int32 [16384], P(('runs', 'gx', 'gy', 'gz')), parts along dimension 0, may hold values from 0 to 15, as said below
- row_count: int32 [16384], P(('runs', 'gx', 'gy', 'gz')), parts along dimension 0, may hold values from 1 to 128
- row_block: int32 [16384], P(('runs', 'gx', 'gy', 'gz')), parts along dimension 0, may hold values from 0 to 8191
- offsets: float32 [3, 16384, 128], P(None, ('runs', 'gx', 'gy', 'gz')), parts along dimension 1, may hold values from 0 to 2
- particle_mass: float32 [16384, 128], P(('runs', 'gx', 'gy', 'gz')), parts along dimension 0, may hold values from 0.25 to 4
- particle_velocity: float32 [3, 16384, 128], P(None, ('runs', 'gx', 'gy', 'gz')), parts along dimension 1, may hold values from -18 to 18
- material: int32 [64, 128, 256], P(('runs', 'gx'), 'gy', 'gz'), parts along dimension 0, may hold values from 0 to 7
- stiffness: float32 [8], replicated, may hold values from 0.02 to 0.16
Outputs:
- node_mass: float32 [64, 128, 256], P(('runs', 'gx'), 'gy', 'gz'), parts along dimension 0
- node_velocity: float32 [3, 64, 128, 256], P(None, ('runs', 'gx'), 'gy', 'gz'), parts along dimension 1
There are 2 independent parts, one for each index of `runs`. A program takes and returns all parts, laid end to end along the dimension named above; an argument that names none is the same for every part. Nothing has to cross between parts.
Inputs may be any that keep to these rules, and one draw needn't show every extreme that they name: row_owner is the index over gx, gy, gz together (gx slowest) of the row's holder or of a device next to it along exactly one of the three axes; no holder gives more than 4 rows to one other device, and in every draw some holder gives exactly 4 rows to one neighbour.
All inputs are finite; a program needn't handle non-finite values.
Results may differ from a plain program's by a relative error of at most 0.0003.
Values sent between devices are 32-bit elements; how exact they have to be, the bound alone decides.
A program may use at most 64 MiB of HBM per device.

v0:
```python
import jax
import jax.numpy as jnp
from jax import lax
from jax.sharding import PartitionSpec as P

CAP = 4


gravity_step = 0.05


def extended(block, sides, width):
    for axis, dim in sides:
        count = lax.axis_size(axis)
        forward = [(i, i + 1) for i in range(count - 1)]
        backward = [(target, source) for source, target in forward]
        low = lax.ppermute(
            lax.slice_in_dim(block, block.shape[dim] - width, None, axis=dim), axis, forward
        )
        high = lax.ppermute(lax.slice_in_dim(block, 0, width, axis=dim), axis, backward)
        block = jnp.concatenate([low, block, high], axis=dim)
    return block


def spline(positions):
    node_step = jnp.arange(4).astype(jnp.float32)[:, None]
    distance = jnp.abs(positions[..., None, :] + 0.5 - node_step)
    inside_part = 0.75 - distance * distance
    outer_part = 0.5 * (1.5 - distance) * (1.5 - distance)
    return jnp.where(distance < 0.5, inside_part, jnp.where(distance < 1.5, outer_part, 0.0))


def patches(positions, masses, speeds):
    row_total = masses.shape[0]
    slot_total = masses.shape[1]
    weight_x = spline(positions[0])
    weight_y = spline(positions[1])
    weight_z = spline(positions[2])
    carried = jnp.stack([masses, masses * speeds[0], masses * speeds[1], masses * speeds[2]], 1)
    left_part = (weight_x[:, :, None, :] * weight_y[:, None, :, :]).reshape(
        row_total, 16, slot_total
    )
    right_part = (carried[:, :, None, :] * weight_z[:, None, :, :]).reshape(
        row_total, 16, slot_total
    )
    stencil = jnp.einsum("nip,njp->nij", left_part, right_part, precision=lax.Precision.HIGHEST)
    return stencil.reshape(row_total, 4, 4, 4, 4)


def scatter_rows(grid_flat, stencil, blocks, shape_ext):
    ext_x, ext_y, ext_z = shape_ext
    half_y = (ext_y - 2) // 2
    half_z = (ext_z - 2) // 2
    node_steps = jnp.arange(4, dtype=jnp.int32)
    base_x = 2 * (blocks // (half_y * half_z))
    base_y = 2 * (blocks // half_z % half_y)
    base_z = 2 * (blocks % half_z)
    index_x = base_x[:, None, None, None, None] + node_steps[None, :, None, None, None]
    index_y = base_y[:, None, None, None, None] + node_steps[None, None, :, None, None]
    channel = node_steps[None, None, None, :, None]
    index_z = base_z[:, None, None, None, None] + node_steps[None, None, None, None, :]
    flat_index = ((channel * ext_x + index_x) * ext_y + index_y) * ext_z + index_z
    return grid_flat.at[flat_index.reshape(-1)].add(stencil.reshape(-1))


def fold_rim(padded, axis_dim):
    length = padded.shape[axis_dim]
    inner_part = lax.slice_in_dim(padded, 2, length - 2, axis=axis_dim)
    low_rim = lax.slice_in_dim(padded, 0, 1, axis=axis_dim)
    high_rim = lax.slice_in_dim(padded, length - 1, length, axis=axis_dim)
    first_layer = lax.slice_in_dim(inner_part, 0, 1, axis=axis_dim) + low_rim
    last_layer = lax.slice_in_dim(inner_part, length - 5, length - 4, axis=axis_dim) + high_rim
    middle = lax.slice_in_dim(inner_part, 1, length - 5, axis=axis_dim)
    return jnp.concatenate([first_layer, middle, last_layer], axis=axis_dim)


def per_device(
    row_owner, row_count, row_block, offsets, particle_mass, particle_velocity, material, stiffness
):
    size_y = lax.axis_size("gy")
    size_z = lax.axis_size("gz")
    coord_x = lax.axis_index("gx")
    coord_y = lax.axis_index("gy")
    coord_z = lax.axis_index("gz")
    myself = (coord_x * size_y + coord_y) * size_z + coord_z
    row_total, slot_total = particle_mass.shape
    span_x, span_y, span_z = material.shape
    shape_ext = (span_x + 2, span_y + 2, span_z + 2)
    live_slots = (
        lax.broadcasted_iota(jnp.int32, (row_total, slot_total), 1) < row_count[:, None]
    ).astype(jnp.float32)
    live_mass = particle_mass * live_slots
    steps_table = jnp.array([-size_y * size_z, size_y * size_z, -size_z, size_z, -1, 1], jnp.int32)
    heading = row_owner - myself
    matches = (heading[:, None] == steps_table[None, :]).astype(jnp.int32)
    moving = jnp.sum(matches, 1) > 0
    direction = jnp.sum(matches * jnp.arange(6, dtype=jnp.int32)[None, :], 1)
    earlier = jnp.cumsum(matches, 0) - matches
    slot_rank = jnp.sum(earlier * matches, 1)
    staying = (row_owner == myself).astype(jnp.float32)
    block_value = jnp.broadcast_to(
        row_block.astype(jnp.float32)[None, :, None], (1, row_total, slot_total)
    )
    grid_flat = jnp.zeros((4 * shape_ext[0] * shape_ext[1] * shape_ext[2],), jnp.float32)
    stencil = patches(offsets, live_mass * staying[:, None], particle_velocity)
    grid_flat = scatter_rows(grid_flat, stencil, row_block, shape_ext)
    payload = jnp.concatenate([offsets, live_mass[None], particle_velocity, block_value], 0)
    channels = payload.shape[0]
    target_slot = jnp.where(moving, direction * CAP + slot_rank, 6 * CAP)
    outbox = (
        jnp.zeros((channels, 6 * CAP, slot_total), jnp.float32)
        .at[:, target_slot]
        .set(payload, mode="drop")
    )
    across_x = extended(outbox[:, 0 : 2 * CAP], (("gx", 1),), CAP)
    across_y = extended(outbox[:, 2 * CAP : 4 * CAP], (("gy", 1),), CAP)
    across_z = extended(outbox[:, 4 * CAP : 6 * CAP], (("gz", 1),), CAP)
    arrived = jnp.concatenate(
        [
            across_x[:, :CAP],
            across_x[:, 3 * CAP :],
            across_y[:, :CAP],
            across_y[:, 3 * CAP :],
            across_z[:, :CAP],
            across_z[:, 3 * CAP :],
        ],
        1,
    )
    arrived_blocks = arrived[channels - 1, :, 0].astype(jnp.int32)
    arrived_stencil = patches(arrived[0:3], arrived[3], arrived[4:7])
    grid_flat = scatter_rows(grid_flat, arrived_stencil, arrived_blocks, shape_ext)
    node_grid = grid_flat.reshape((4,) + shape_ext)
    widened = extended(node_grid, (("gx", 1), ("gy", 2), ("gz", 3)), 1)
    summed = fold_rim(fold_rim(fold_rim(widened, 1), 2), 3)
    node_mass = summed[0]
    velocity = summed[1:] / jnp.maximum(node_mass, 1.0)[None]
    padded = extended(velocity, (("gx", 1), ("gy", 2), ("gz", 3)), 1)
    beside = padded[:, 2:, 1:-1, 1:-1] + padded[:, :-2, 1:-1, 1:-1]
    beside = beside + padded[:, 1:-1, 2:, 1:-1] + padded[:, 1:-1, :-2, 1:-1]
    beside = beside + padded[:, 1:-1, 1:-1, 2:] + padded[:, 1:-1, 1:-1, :-2]
    laplace = beside - 6.0 * velocity
    lookup = material[None] == jnp.arange(stiffness.shape[0], dtype=jnp.int32)[:, None, None, None]
    node_stiff = jnp.sum(jnp.where(lookup, stiffness[:, None, None, None], 0.0), 0)
    updated = velocity + node_stiff[None] * laplace
    vertical = updated[2] - gravity_step
    bottom = coord_z * span_z + lax.broadcasted_iota(jnp.int32, (1, 1, span_z), 2) == 0
    vertical = jnp.where(bottom, jnp.maximum(vertical, 0.0), vertical)
    node_velocity = jnp.stack([updated[0], updated[1], vertical], 0)
    return (node_mass, node_velocity)


def solution(mesh):
    placed = (
        P(("runs", "gx", "gy", "gz")),
        P(("runs", "gx", "gy", "gz")),
        P(("runs", "gx", "gy", "gz")),
        P(None, ("runs", "gx", "gy", "gz"), None),
        P(("runs", "gx", "gy", "gz"), None),
        P(None, ("runs", "gx", "gy", "gz"), None),
        P(("runs", "gx"), "gy", "gz"),
        P(),
    )
    return jax.shard_map(
        per_device,
        mesh=mesh,
        in_specs=placed,
        out_specs=(P(("runs", "gx"), "gy", "gz"), P(None, ("runs", "gx"), "gy", "gz")),
        check_vma=False,
    )
```

profile of v0, /device:TPU:0, one launch (start us, length us, event | category | flops | bytes accessed | tf_op | source)
XLA Modules:
  0.0 985.9 jit_solution(10344371398026067967)
XLA Ops:
  0.7 0.8 compare_convert_fusion.2
  2.8 1.4 fusion.75
  4.2 0.7 compare_convert_fusion.1
  4.9 1.8 reduce-window.6
  7.1 0.8 fusion.54
  7.9 2.2 fusion.31
  10.4 1.2 copy.46
  11.6 14.8 %scatter_fusion = f32[8,24,128]{2,0,1:T(8,128)S(1)} fusion(f32[8,24,128]{2,0,1:T(8,128)S(1)} %broadcast_in_dim.41, s32[512]{0:T(512)S(1)} %bitcast.94, f32[512,8,128]{2,1,0:T(8,128)S(1)} %copy.46), kind=kCustom, calls=%fused_computation.1 | custom fusion | bytes 6293504 | tf_op jit(solution)/shard_map/scatter | solution.py:113
  27.1 5.5 collective-permute-start
  32.6 1.3 collective-permute-start.1
  33.9 4.0 collective-permute-start.2
  37.9 1.3 collective-permute-start.3
  39.2 1.9 collective-permute-start.4
  41.1 0.8 iota_add_fusion.2
  41.9 0.9 iota_add_fusion
  42.8 1.3 add_multiply_fusion.1
  44.2 2.3 add_multiply_fusion
  46.5 12.5 %broadcast_add_fusion = s32[512,4,4,4,4]{4,3,2,1,0:T(4,128)} fusion(s32[512,4]{1,0:T(8,128)S(1)} %get-tuple-element.60, s32[512,4,4,4]{3,2,1,0:T(4,128)S(1)} %add_multiply_fusion), kind=kLoop, calls=%fused_computation.3 | loop fusion | flops 131072 | bytes 663552 | tf_op jit(solution)/shard_map/add | solution.py:62
  59.0 28.0 %add.461 = s32[131072,1]{0,1:T(1,128)S(1)} reshape(s32[512,4,4,4,4]{4,3,2,1,0:T(4,128)} %broadcast_add_fusion) | data formatting | bytes 1048576 | tf_op jit(solution)/shard_map/add | solution.py:62
  88.3 2.4 fusion.16
  90.7 2.2 broadcast_multiply_fusion
  93.0 8.4 fusion.76
  101.4 3.2 reshape.579
  104.6 753.3 %scatter_custom_fusion = f32[343200]{0:T(1024)S(1)} fusion(s32[131072]{0:T(1024)S(1)} %bitcast.83, f32[131072]{0:T(1024)S(1)} %reshape.579, f32[]{:T(128)} %constant.120.clone.1), kind=kCustom, calls=%fused_computation.77 | custom fusion | flops 131072 | bytes 1372804 | tf_op jit(solution)/shard_map/scatter-add | solution.py:63
  858.0 1.3 collective-permute-start.5
  859.3 0.7 constant_dynamic-update-slice_fusion.5
  860.0 0.7 constant_dynamic-update-slice_fusion.4
  860.7 0.7 constant_dynamic-update-slice_fusion.3
  861.5 0.7 constant_dynamic-update-slice_fusion.2
  862.2 0.7 constant_dynamic-update-slice_fusion.1
  864.5 0.9 add.494
  866.3 37.9 %scatter_fusion.1 = f32[343200]{0:T(1024)S(1)} fusion(f32[343200]{0:T(1024)S(1)} %scatter_custom_fusion, s32[6144]{0:T(1024)S(1)} %bitcast.87, f32[6144]{0:T(1024)S(1)} %reshape.595), kind=kCustom, calls=%fused_computation.2 | custom fusion | flops 6144 | bytes 98304 | tf_op jit(solution)/shard_map/scatter-add | solution.py:63
  904.1 3.2 reshape.574
  907.3 1.1 fusion.70
  908.4 4.6 collective-permute-start.6
  913.0 1.3 collective-permute-start.7
  914.3 5.9 collective-permute-done.6
  920.3 2.1 constant_dynamic-update-slice_fusion.7
  922.4 2.3 collective-permute-done.7
  924.8 1.3 collective-permute-start.9
  926.1 5.3 collective-permute-start.8
  931.4 1.5 collective-permute-done.8
  933.5 2.3 fusion.68
  935.8 2.7 copy.52
  938.5 1.3 collective-permute-start.11
  939.8 2.7 copy.51
  942.5 4.2 collective-permute-start.10
  946.7 2.6 copy.54
  949.4 2.6 copy.53
  952.0 3.7 pad_maximum_fusion.1
  955.9 1.3 copy-done
  959.3 0.9 slice_add_fusion.1
  960.5 0.9 maximum_bitcast_fusion.1
  961.9 1.3 collective-permute-start.12
  963.2 4.6 collective-permute-start.13
  968.4 1.5 collective-permute-done.13
  970.0 1.3 collective-permute-start.14
  971.3 4.5 collective-permute-start.15
  976.2 1.1 collective-permute-done.15
  978.2 1.3 collective-permute-start.17
  979.9 1.3 collective-permute-start.16
  981.7 1.2 collective-permute-done.16
  983.5 0.9 fusion.21
  984.5 0.9 pad_maximum_fusion.26
  (101 shorter events, 13.6 us)
Async XLA Ops:
  0.6 9.6 copy-start.3
  0.6 9.6 copy-start.2
  27.1 830.9 %collective-permute-start = (f32[8,4,128]{2,0,1:T(8,128)}, f32[8,4,128]{2,0,1:T(8,128)}, u32[]{:S(2)}, u32[]{:S(2)}) collective-permute-start(f32[8,4,128]{2,0,1:T(8,128)} %get-tuple-element.43), channel_id=1, source_target_pairs={{0,4},{4,8},{8,12},{1,5},{5,9},{9,13},{2,6},{6,10},{10,14},{3,7},{... | collective-permute-start | bytes 49160 | tf_op jit(solution)/shard_map/ppermute | solution.py:17
  32.6 827.4 %collective-permute-start.1 = (f32[8,4,128]{2,0,1:T(8,128)}, f32[8,4,128]{2,0,1:T(8,128)}, u32[]{:S(2)}, u32[]{:S(2)}) collective-permute-start(f32[8,4,128]{2,0,1:T(8,128)} %get-tuple-element.42), channel_id=1, source_target_pairs={{4,0},{8,4},{12,8},{5,1},{9,5},{13,9},{6,2},{10,6},{14,10},{7,3},{... | collective-permute-start | bytes 49160 | tf_op jit(solution)/shard_map/ppermute | solution.py:20
  33.9 826.9 %collective-permute-start.2 = (f32[8,4,128]{2,0,1:T(8,128)}, f32[8,4,128]{2,0,1:T(8,128)}, u32[]{:S(2)}, u32[]{:S(2)}) collective-permute-start(f32[8,4,128]{2,0,1:T(8,128)} %get-tuple-element.41), channel_id=1, source_target_pairs={{0,2},{1,3},{4,6},{5,7},{8,10},{9,11},{12,14},{13,15},{16,18},{17,... | collective-permute-start | bytes 49160 | tf_op jit(solution)/shard_map/ppermute | solution.py:17
  37.9 823.6 %collective-permute-start.3 = (f32[8,4,128]{2,0,1:T(8,128)S(1)}, f32[8,4,128]{2,0,1:T(8,128)}, u32[]{:S(2)}, u32[]{:S(2)}) collective-permute-start(f32[8,4,128]{2,0,1:T(8,128)S(1)} %get-tuple-element.40), channel_id=1, source_target_pairs={{2,0},{3,1},{6,4},{7,5},{10,8},{11,9},{14,12},{15,13},{18,16},{19,... | collective-permute-start | bytes 49160 | tf_op jit(solution)/shard_map/ppermute | solution.py:20
  39.2 823.0 %collective-permute-start.4 = (f32[8,4,128]{2,0,1:T(8,128)S(1)}, f32[8,4,128]{2,0,1:T(8,128)}, u32[]{:S(2)}, u32[]{:S(2)}) collective-permute-start(f32[8,4,128]{2,0,1:T(8,128)S(1)} %get-tuple-element.39), channel_id=1, source_target_pairs={{0,1},{2,3},{4,5},{6,7},{8,9},{10,11},{12,13},{14,15},{16,17},{18,... | collective-permute-start | bytes 49160 | tf_op jit(solution)/shard_map/ppermute | solution.py:17
  41.1 5.4 copy-start.11
  59.0 28.5 %copy-start.4 = (f32[512,1,128]{2,0,1:T(8,128)S(1)}, f32[512,1,128]{2,0,1:T(8,128)}, u32[]{:S(2)}) copy-start(f32[512,1,128]{2,0,1:T(8,128)} %get-tuple-element.21) | copy-start | bytes 786436
  59.0 28.5 %copy-start.5 = (f32[512,1,128]{2,0,1:T(8,128)S(1)}, f32[512,1,128]{2,0,1:T(8,128)}, u32[]{:S(2)}) copy-start(f32[512,1,128]{2,0,1:T(8,128)} %get-tuple-element.29) | copy-start | bytes 786436
  101.4 762.2 %copy-start.12 = (s32[4]{0:T(128)S(1)}, s32[4]{0:T(128)}, u32[]{:S(2)}) copy-start(s32[4]{0:T(128)} %copy-done.11) | copy-start | bytes 52
  858.0 4.9 collective-permute-start.5
  908.4 11.8 %collective-permute-start.6 = (f32[4,1,66,130]{3,2,1,0:T(8,128)S(1)}, f32[4,1,66,130]{3,2,1,0:T(8,128)S(1)}, u32[]{:S(2)}, u32[]{:S(2)}) collective-permute-start(f32[4,1,66,130]{3,2,1,0:T(8,128)S(1)} %get-tuple-element.12), channel_id=1, source_target_pairs={{0,4},{4,8},{8,12},{1,5},{5,9},{9,13},{2,6},{6,10},{10,14},{3,7},{... | collective-permute-start | bytes 411848 | tf_op jit(solution)/shard_map/ppermute | solution.py:17
  913.0 11.6 %collective-permute-start.7 = (f32[4,1,66,130]{3,2,1,0:T(8,128)S(1)}, f32[4,1,66,130]{3,2,1,0:T(8,128)S(1)}, u32[]{:S(2)}, u32[]{:S(2)}) collective-permute-start(f32[4,1,66,130]{3,2,1,0:T(8,128)S(1)} %get-tuple-element.11), channel_id=1, source_target_pairs={{4,0},{8,4},{12,8},{5,1},{9,5},{13,9},{6,2},{10,6},{14,10},{7,3},{... | collective-permute-start | bytes 411848 | tf_op jit(solution)/shard_map/ppermute | solution.py:20
  924.8 6.6 collective-permute-start.9
  926.1 6.8 collective-permute-start.8
  931.4 1.9 copy-start.6
  932.9 0.6 copy-start.8
  938.5 8.2 collective-permute-start.11
  942.5 6.9 collective-permute-start.10
  952.0 3.9 copy-start.7
  952.0 3.9 copy-start.9
  955.7 1.5 copy-start
  955.7 2.0 copy-start.1
  961.4 14.4 %copy-start.10 = (s32[8,64,128]{2,1,0:T(8,128)S(1)}, s32[8,64,128]{2,1,0:T(8,128)}, u32[]{:S(2)}) copy-start(s32[8,64,128]{2,1,0:T(8,128)} %param.15) | copy-start | bytes 786436
  961.4 14.4 %copy-start.13 = (f32[8]{0:T(128)S(1)}, f32[8]{0:T(128)}, u32[]{:S(2)}) copy-start(f32[8]{0:T(128)} %param.16) | copy-start | bytes 100
  961.9 6.5 collective-permute-start.12
  963.2 6.8 collective-permute-start.13
  970.0 6.2 collective-permute-start.14
  971.3 6.0 collective-permute-start.15
  978.2 3.0 collective-permute-start.17
  979.9 3.1 collective-permute-start.16
where the time goes:
time: 991 us; the launch traced here: 986 us
  other arithmetic  835 us (84%)
  local copies, waits for them, and re-layouts  78 us (8%)
  starting transfers between devices  47.5 us (5%)
  waiting for transfers between devices  14.2 us (1%)
    scatter-add x2, other arithmetic, scatter_rows(): return grid_flat.at[flat_index.reshape(-1)].add(stencil.reshape(-1))  791 us
    ppermute x9, starting transfers between devices, extended(): lax.ppermute(lax.slice_in_dim(block, block.shape[dim] - width, None, axis...  35.9 us
    add x2, local copies, waits for them, and re-layouts, scatter_rows(): ((channel * ext_x + index_x) * ext_y + index_y) * ext_z + index_z  28.8 us
  transfers between devices with their start and end apart: 18, of which 7 were waited for; matrix products, arithmetic and copies ran while one was open for 84% of the time, Pallas kernels for 0%

commit v1 on v0

v1 whole, which is shorter than its diff:
```python
import functools

import jax
import jax.numpy as jnp
from jax import lax
from jax.experimental import pallas as pl
from jax.experimental.pallas import tpu as pltpu
from jax.sharding import PartitionSpec as P

CAP = 4
LANES = 128
gravity_step = 0.05
AXES = ("gx", "gy", "gz")
VMEM_LIMIT = 48 * 1024 * 1024


def spline(distance):
    distance = jnp.abs(distance)
    inside_part = 0.75 - distance * distance
    rest = jnp.maximum(1.5 - distance, 0.0)
    return jnp.where(distance < 0.5, inside_part, 0.5 * rest * rest)


def neighbours(counts):
    found = []
    for axis in AXES:
        here = lax.axis_index(axis)
        low = here > 0
        high = here < counts[axis] - 1
        found.append((axis, here - 1, low, high))
        found.append((axis, here + 1, high, low))
    return found


def greet(sides):
    barrier = pltpu.get_barrier_semaphore()
    total = 0
    for axis, target, there, _ in sides:
        @pl.when(there)
        def _():
            pl.semaphore_signal(
                barrier, inc=1, device_id={axis: target}, device_id_type=pl.DeviceIdType.MESH
            )
        total = total + there.astype(jnp.int32)
    pl.semaphore_wait(barrier, total)


def remote(source, target_ref, send_sem, recv_sem, axis, target):
    return pltpu.make_async_remote_copy(
        src_ref=source,
        dst_ref=target_ref,
        send_sem=send_sem,
        recv_sem=recv_sem,
        device_id={axis: target},
        device_id_type=pl.DeviceIdType.MESH,
    )


def rows_kernel(
    counts, owner_ref, count_ref, block_ref, offs_ref, mass_ref, vel_ref, box_ref, out_box, send_sem, recv_sem
):
    rows = mass_ref.shape[0]
    size_y, size_z = counts["gy"], counts["gz"]
    myself = (lax.axis_index("gx") * size_y + lax.axis_index("gy")) * size_z + lax.axis_index("gz")
    sides = neighbours(counts)
    box_ref[...] = jnp.zeros_like(box_ref)
    heading = owner_ref[...] - myself
    shape = heading.shape
    place = lax.broadcasted_iota(jnp.int32, shape, 0) * LANES + lax.broadcasted_iota(jnp.int32, shape, 1)
    lane = lax.broadcasted_iota(jnp.int32, (1, LANES), 1)
    steps = (-size_y * size_z, size_y * size_z, -size_z, size_z, -1, 1)
    left = [jnp.where(heading == step, place, rows) for step in steps]
    for slot in range(CAP):
        for way in range(6):
            first = jnp.min(left[way])
            left[way] = jnp.where(left[way] == first, rows, left[way])
            valid = first < rows
            row = jnp.minimum(first, rows - 1)
            live = jnp.where(valid, count_ref[row], 0)
            for j in range(3):
                out_box[way, slot, pl.ds(j, 1), :] = offs_ref[j, pl.ds(row, 1), :]
                out_box[way, slot, pl.ds(4 + j, 1), :] = vel_ref[j, pl.ds(row, 1), :]
            out_box[way, slot, pl.ds(3, 1), :] = jnp.where(lane < live, mass_ref[pl.ds(row, 1), :], 0.0)
            block = jnp.where(valid, block_ref[row], 0).astype(jnp.float32)
            out_box[way, slot, pl.ds(7, 1), :] = jnp.full((1, LANES), block, jnp.float32)
    greet(sides)
    copies = [
        remote(out_box.at[way], box_ref.at[way], send_sem.at[way], recv_sem.at[way], axis, target)
        for way, (axis, target, _, _) in enumerate(sides)
    ]
    for way, (_, _, there, _) in enumerate(sides):
        pl.when(there)(copies[way].start)
    for way, (_, _, there, other) in enumerate(sides):
        pl.when(there)(copies[way].wait_send)
        pl.when(other)(copies[way].wait_recv)


def deposit_kernel(
    half_y, half_z, planes, me_ref, owner_ref, count_ref, block_ref, came_ref,
    offs_ref, mass_ref, vel_ref, box_ref, out_ref, grid_ref, wx_ref, yk_ref, wz_ref,
):
    rows = mass_ref.shape[0]
    came = box_ref.shape[0]
    sub = lax.broadcasted_iota(jnp.int32, (8, LANES), 0)
    lane = lax.broadcasted_iota(jnp.int32, (8, LANES), 1)
    myself = me_ref[0]
    zero8 = jnp.zeros((8, LANES), jnp.float32)

    def clear(i, carry):
        grid_ref[i] = jnp.zeros(grid_ref.shape[1:], jnp.float32)
        return carry

    lax.fori_loop(0, grid_ref.shape[0], clear, 0)

    def fill(base, ox, oy, oz, carried):
        for a in range(4):
            wx_ref[pl.ds(base * 4 + a, 8, stride=4), :] = spline(ox + (0.5 - a))
            wy = spline(oy + (0.5 - a))
            for k in range(4):
                yk_ref[pl.ds(base * 16 + a * 4 + k, 8, stride=16), :] = wy * carried[k]
            wz_ref[pl.ds(base * 8 + a, 8, stride=8), :] = spline(oz + (0.5 - a))
            wz_ref[pl.ds(base * 8 + 4 + a, 8, stride=8), :] = zero8

    def prepare(i, carry):
        base = pl.multiple_of(i * 8, 8)
        live = jnp.zeros((8, LANES), jnp.int32)
        for s in range(8):
            count = jnp.where(owner_ref[base + s] == myself, count_ref[base + s], 0)
            live = jnp.where(sub == s, count, live)
        at = pl.ds(base, 8)
        mass = jnp.where(lane < live, mass_ref[at, :], 0.0)
        carried = [mass] + [mass * vel_ref[j, at, :] for j in range(3)]
        fill(base, offs_ref[0, at, :], offs_ref[1, at, :], offs_ref[2, at, :], carried)
        return carry

    lax.fori_loop(0, rows // 8, prepare, 0)
    for group in range(came // 64):
        part = [box_ref[pl.ds(group * 64 + c, 8, stride=8), :] for c in range(8)]
        carried = [part[3]] + [part[3] * part[4 + j] for j in range(3)]
        fill(rows + group * 8, part[0], part[1], part[2], carried)

    def stencil(row):
        parts = []
        yk = yk_ref[pl.ds(pl.multiple_of(row * 16, 16), 16), :]
        for a in range(4):
            parts.append(yk * wx_ref[pl.ds(row * 4 + a, 1), :])
        left = jnp.concatenate(parts, 0)
        high = left.astype(jnp.bfloat16)
        low = (left - high.astype(jnp.float32)).astype(jnp.bfloat16)
        wz = wz_ref[pl.ds(pl.multiple_of(row * 8, 8), 8), :]
        zhigh = wz.astype(jnp.bfloat16)
        zlow = (wz - zhigh.astype(jnp.float32)).astype(jnp.bfloat16)
        lhs = jnp.concatenate([high, low, high], 1)
        rhs = jnp.concatenate([zhigh, zhigh, zlow], 1)
        rhs = jnp.concatenate([rhs, jnp.zeros((LANES - 8, 3 * LANES), jnp.bfloat16)], 0)
        return lax.dot_general(lhs, rhs, (((1,), (1,)), ((), ())), preferred_element_type=jnp.float32)

    def place(block, sums):
        base_x = 2 * lax.div(block, half_y * half_z)
        rest = lax.rem(block, half_y * half_z)
        base_y = lax.div(rest, half_z)
        base_z = lax.rem(rest, half_z)
        layer = jnp.where(base_z == 0, planes, jnp.where(base_z == half_z - 1, 2 * planes, 0))
        shift = lax.rem(2 * base_z + LANES - 1, LANES)
        sums = pltpu.roll(sums, shift, 1)
        at = pl.ds(pl.multiple_of(base_y * 8, 8), 16)
        for a in range(4):
            spot = layer + base_x + a
            grid_ref[spot, at, :] = grid_ref[spot, at, :] + sums[a * 16 : a * 16 + 16]

    def row_group(i, carry):
        results = [stencil(i * 8 + s) for s in range(8)]
        for s in range(8):
            place(block_ref[i * 8 + s], results[s])
        return carry

    lax.fori_loop(0, rows // 8, row_group, 0)

    def came_group(i, carry):
        results = [stencil(rows + i * 8 + s) for s in range(8)]
        for s in range(8):
            place(came_ref[i * 8 + s], results[s])
        return carry

    lax.fori_loop(0, came // 64, came_group, 0)

    def finish(i, carry):
        at = pl.ds(pl.multiple_of(i * 8, 8), 8)
        low, high = zero8, zero8
        for x in range(planes):
            first = grid_ref[planes + x, at, :]
            last = grid_ref[2 * planes + x, at, :]
            main = grid_ref[x, at, :] + jnp.where(lane < LANES - 1, first, 0.0) + jnp.where(lane > 0, last, 0.0)
            out_ref[x, at, :] = main
            low = jnp.where(lane == x, pltpu.roll(first, x + 1, 1), low)
            low = jnp.where(lane == 16 + x, pltpu.roll(main, 16 + x, 1), low)
            high = jnp.where(lane == x, pltpu.roll(last, x, 1) if x else last, high)
            high = jnp.where(lane == 16 + x, pltpu.roll(main, 17 + x, 1), high)
        out_ref[planes, at, :] = low
        out_ref[planes + 1, at, :] = high
        return carry

    lax.fori_loop(0, out_ref.shape[1] // 8, finish, 0)


def halo_kernel(counts, grid_in, out_ref, z_box, y_box, x_box, edge_ref, edge_box, send_sem, recv_sem):
    planes = out_ref.shape[0] - 2
    tall = out_ref.shape[1]
    sides = neighbours(counts)
    lane = lax.broadcasted_iota(jnp.int32, (8, LANES), 1)
    z_box[...] = jnp.zeros_like(z_box)
    y_box[...] = jnp.zeros_like(y_box)
    x_box[...] = jnp.zeros_like(x_box)
    edge_box[...] = jnp.zeros_like(edge_box)
    greet(sides)

    def exchange(ways, sources, targets, sems):
        copies = []
        for way, source, target_ref, sem in zip(ways, sources, targets, sems):
            axis, target, there, other = sides[way]
            copy = remote(source, target_ref, send_sem.at[sem], recv_sem.at[sem], axis, target)
            pl.when(there)(copy.start)
            copies.append((copy, there, other))
        for copy, there, other in copies:
            pl.when(there)(copy.wait_send)
            pl.when(other)(copy.wait_recv)

    exchange((4, 5), (grid_in.at[planes], grid_in.at[planes + 1]), (z_box.at[0], z_box.at[1]), (4, 5))

    def add_z(i, carry):
        at = pl.ds(pl.multiple_of(i * 8, 8), 8)
        above, below = z_box[0, at, :], z_box[1, at, :]
        for x in range(planes):
            main = grid_in[x, at, :]
            main = main + jnp.where(lane == LANES - 1, pltpu.roll(above, LANES - 1 - x, 1), 0.0)
            down = pltpu.roll(below, LANES - x, 1) if x else below
            out_ref[x, at, :] = main + jnp.where(lane == 0, down, 0.0)
        out_ref[planes, at, :] = grid_in[planes, at, :] + pltpu.roll(below, LANES - 16, 1)
        out_ref[planes + 1, at, :] = grid_in[planes + 1, at, :] + pltpu.roll(above, LANES - 16, 1)
        return carry

    lax.fori_loop(0, tall // 8, add_z, 0)
    first, last = pl.ds(0, 8), pl.ds(tall - 8, 8)
    exchange(
        (2, 3),
        (out_ref.at[:, first, :], out_ref.at[:, last, :]),
        (y_box.at[0], y_box.at[1]),
        (2, 3),
    )
    for x in range(planes + 2):
        out_ref[x, last, :] = out_ref[x, last, :] + y_box[0, x]
        out_ref[x, first, :] = out_ref[x, first, :] + y_box[1, x]

    def pack(i, carry):
        at = pl.ds(pl.multiple_of(i * 8, 8), 8)
        edge_ref[at, :] = jnp.where(lane < 16, out_ref[planes, at, :], pltpu.roll(out_ref[planes + 1, at, :], 16, 1))
        return carry

    lax.fori_loop(0, tall // 8, pack, 0)
    exchange(
        (0, 1, 0, 1),
        (out_ref.at[pl.ds(0, 2)], out_ref.at[pl.ds(planes - 2, 2)], edge_ref, edge_ref),
        (x_box.at[0], x_box.at[1], edge_box.at[0], edge_box.at[1]),
        (0, 1, 6, 7),
    )

    def add_x(i, carry):
        at = pl.ds(pl.multiple_of(i * 8, 8), 8)
        for p in range(2):
            out_ref[planes - 2 + p, at, :] = out_ref[planes - 2 + p, at, :] + x_box[0, p, at, :]
            out_ref[p, at, :] = out_ref[p, at, :] + x_box[1, p, at, :]
        above, below = edge_box[0, at, :], edge_box[1, at, :]
        for side in range(2):
            value = out_ref[planes + side, at, :]
            start = 16 * side
            value = value + jnp.where(
                lane == planes - 2, pltpu.roll(above, (planes - 2 - start) % LANES, 1), 0.0
            )
            value = value + jnp.where(
                lane == 1, pltpu.roll(below, (1 - (planes - 1) - start) % LANES, 1), 0.0
            )
            out_ref[planes + side, at, :] = value
        return carry

    lax.fori_loop(0, tall // 8, add_x, 0)


def update_kernel(counts, grid_ref, mat_ref, stiff_ref, mass_ref, vel_ref, v_ref, z_ref):
    span_x, span_y, span_z = mass_ref.shape
    planes = span_x + 2
    there = [side[2].astype(jnp.float32) for side in neighbours(counts)]
    lane = lax.broadcasted_iota(jnp.int32, (span_y, LANES), 1)
    bottom = jnp.logical_and(lane == 0, jnp.logical_not(lax.axis_index("gz") > 0))

    def speeds(x, start, length, scale):
        def read(k):
            if length == 1:
                return grid_ref[x, pl.ds(start * 4 + k, 1), :]
            return grid_ref[x, pl.ds(start * 4 + k, length, stride=4), :]

        under = scale / jnp.maximum(read(0), 1.0)
        return [read(1 + j) * under for j in range(3)]

    def fill(x, carry):
        scale = jnp.where(x == 0, there[0], jnp.where(x == planes - 1, there[1], 1.0))
        for j, value in enumerate(speeds(x, 1, span_y, scale)):
            v_ref[j, x, pl.ds(8, span_y), :] = value
        for j, value in enumerate(speeds(x, 0, 1, there[2])):
            v_ref[j, x, pl.ds(7, 1), :] = value
        for j, value in enumerate(speeds(x, span_y + 1, 1, there[3])):
            v_ref[j, x, pl.ds(8 + span_y, 1), :] = value
        return carry

    lax.fori_loop(0, planes, fill, 0)
    for side in range(2):
        for j, value in enumerate(speeds(planes + side, 1, span_y, there[4 + side])):
            z_ref[side, j] = value

    def update(x, carry):
        mass_ref[x] = grid_ref[x + 1, pl.ds(4, span_y, stride=4), :]
        material = mat_ref[x]
        stiff = jnp.zeros((span_y, LANES), jnp.float32)
        for m in range(stiff_ref.shape[0]):
            stiff = jnp.where(material == m, stiff_ref[m], stiff)
        for j in range(3):
            value = v_ref[j, x + 1, pl.ds(8, span_y), :]
            beside = v_ref[j, x + 2, pl.ds(8, span_y), :] + v_ref[j, x, pl.ds(8, span_y), :]
            beside = beside + v_ref[j, x + 1, pl.ds(9, span_y), :] + v_ref[j, x + 1, pl.ds(7, span_y), :]
            after = pltpu.roll(z_ref[1, j], LANES - 2 - x, 1)
            before = pltpu.roll(z_ref[0, j], LANES - 1 - x, 1)
            beside = beside + jnp.where(lane == LANES - 1, after, pltpu.roll(value, LANES - 1, 1))
            beside = beside + jnp.where(lane == 0, before, pltpu.roll(value, 1, 1))
            result = value + stiff * (beside - 6.0 * value)
            if j == 2:
                result = result - gravity_step
                result = jnp.where(bottom, jnp.maximum(result, 0.0), result)
            vel_ref[j, x] = result
        return carry

    lax.fori_loop(0, span_x, update, 0)


def per_device(
    counts, row_owner, row_count, row_block, offsets, particle_mass, particle_velocity, material, stiffness
):
    rows = particle_mass.shape[0]
    span_x, span_y, span_z = material.shape
    planes = span_x + 2
    tall = (span_y + 2) * 4
    f32 = jnp.float32
    vmem = pl.BlockSpec(memory_space=pltpu.VMEM)
    smem = pl.BlockSpec(memory_space=pltpu.SMEM)
    myself = (lax.axis_index("gx") * counts["gy"] + lax.axis_index("gy")) * counts["gz"] + lax.axis_index("gz")

    box = pl.pallas_call(
        functools.partial(rows_kernel, counts),
        out_shape=jax.ShapeDtypeStruct((6, CAP, 8, LANES), f32),
        in_specs=[vmem, smem, smem, vmem, vmem, vmem],
        out_specs=vmem,
        scratch_shapes=[
            pltpu.VMEM((6, CAP, 8, LANES), f32),
            pltpu.SemaphoreType.DMA((6,)),
            pltpu.SemaphoreType.DMA((6,)),
        ],
        compiler_params=pltpu.CompilerParams(
            collective_id=0, has_side_effects=True, vmem_limit_bytes=VMEM_LIMIT
        ),
        name="row_exchange",
    )(row_owner.reshape(-1, LANES), row_count, row_block, offsets, particle_mass, particle_velocity)

    came_blocks = box[:, :, 7, 0].reshape(-1).astype(jnp.int32)
    total = rows + 6 * CAP
    grid = pl.pallas_call(
        functools.partial(deposit_kernel, span_y // 2, span_z // 2, planes),
        out_shape=jax.ShapeDtypeStruct((planes + 2, tall, LANES), f32),
        in_specs=[smem] * 5 + [vmem] * 4,
        out_specs=vmem,
        scratch_shapes=[
            pltpu.VMEM((3 * planes, tall, LANES), f32),
            pltpu.VMEM((total * 4, LANES), f32),
            pltpu.VMEM((total * 16, LANES), f32),
            pltpu.VMEM((total * 8, LANES), f32),
        ],
        compiler_params=pltpu.CompilerParams(vmem_limit_bytes=VMEM_LIMIT),
        name="deposit",
    )(
        myself.reshape(1), row_owner, row_count, row_block, came_blocks,
        offsets, particle_mass, particle_velocity, box.reshape(6 * CAP * 8, LANES),
    )

    grid = pl.pallas_call(
        functools.partial(halo_kernel, counts),
        out_shape=jax.ShapeDtypeStruct((planes + 2, tall, LANES), f32),
        in_specs=[vmem],
        out_specs=vmem,
        scratch_shapes=[
            pltpu.VMEM((2, tall, LANES), f32),
            pltpu.VMEM((2, planes + 2, 8, LANES), f32),
            pltpu.VMEM((2, 2, tall, LANES), f32),
            pltpu.VMEM((tall, LANES), f32),
            pltpu.VMEM((2, tall, LANES), f32),
            pltpu.SemaphoreType.DMA((8,)),
            pltpu.SemaphoreType.DMA((8,)),
        ],
        compiler_params=pltpu.CompilerParams(
            collective_id=1, has_side_effects=True, vmem_limit_bytes=VMEM_LIMIT
        ),
        name="halo_sums",
    )(grid)

    return pl.pallas_call(
        functools.partial(update_kernel, counts),
        out_shape=(
            jax.ShapeDtypeStruct((span_x, span_y, span_z), f32),
            jax.ShapeDtypeStruct((3, span_x, span_y, span_z), f32),
        ),
        in_specs=[vmem, vmem, smem],
        out_specs=(vmem, vmem),
        scratch_shapes=[
            pltpu.VMEM((3, planes, span_y + 16, LANES), f32),
            pltpu.VMEM((2, 3, span_y, LANES), f32),
        ],
        compiler_params=pltpu.CompilerParams(vmem_limit_bytes=VMEM_LIMIT),
        name="grid_update",
    )(grid, material, stiffness)


def solution(mesh):
    placed = (
        P(("runs", "gx", "gy", "gz")),
        P(("runs", "gx", "gy", "gz")),
        P(("runs", "gx", "gy", "gz")),
        P(None, ("runs", "gx", "gy", "gz"), None),
        P(("runs", "gx", "gy", "gz"), None),
        P(None, ("runs", "gx", "gy", "gz"), None),
        P(("runs", "gx"), "gy", "gz"),
        P(),
    )
    counts = {axis: mesh.shape[axis] for axis in AXES}
    return jax.shard_map(
        functools.partial(per_device, counts),
        mesh=mesh,
        in_specs=placed,
        out_specs=(P(("runs", "gx"), "gy", "gz"), P(None, ("runs", "gx"), "gy", "gz")),
        check_vma=False,
    )
```

time: 991 us -> 71.3 us (0.07)
  other arithmetic: 835 us -> 0.51 us
  local copies, waits for them, and re-layouts: 78 us -> 5.38 us
  Pallas kernels: 0 us -> 64.3 us
  starting transfers between devices: 47.5 us -> 0 us
  waiting for transfers between devices: 14.2 us -> 0 us
    scatter-add x2 -> x0, other arithmetic: 791 us -> none  [scatter_rows(): return grid_flat.at[flat_index.reshape(-1)].add(stencil.reshape(-1))]
    pallas_call x0 -> x4, Pallas kernels: none -> 64.3 us  [the longest x1 29.1 us: per_device(): pl.pallas_call(functools.partial(deposit_kernel, span_y // 2, span_z // 2...]
    ppermute x18 -> x0, starting transfers between devices: 47.5 us -> none  [the longest x9 35.9 us: extended(): lax.ppermute(lax.slice_in_dim(block, block.shape[dim] - width, None, axis...]
    add x2 -> x0, local copies, waits for them, and re-layouts: 28.8 us -> none  [scatter_rows(): ((channel * ext_x + index_x) * ext_y + index_y) * ext_z + index_z]
    add x12 -> x0, other arithmetic: 17.6 us -> none  [the longest x2 13.1 us: scatter_rows(): ((channel * ext_x + index_x) * ext_y + index_y) * ext_z + index_z]
    scatter x1 -> x0, local copies, waits for them, and re-layouts: 14.8 us -> none  [per_device(): outbox = jnp.zeros((channels, 6 * CAP, slot_total), jnp.float32).at[:, ta...]
    ppermute x18 -> x0, waiting for transfers between devices: 14.2 us -> none  [the longest x9 10 us: extended(): lax.ppermute(lax.slice_in_dim(block, block.shape[dim] - width, None, axis...]
    slice x16 -> x0, local copies, waits for them, and re-layouts: 11.7 us -> none  [the longest x5 5.49 us: extended(): lax.slice_in_dim(block, block.shape[dim] - width, None, axis=dim)]
  transfers between devices with their start and end apart: 18 -> 0, of which waited for: 7 -> 0; matrix products, arithmetic and copies ran while one was open for 84% -> 0% of each run, Pallas kernels for 0% -> 0%
where the time goes in v1:
time: 71.3 us; the launch traced here: 71 us
  Pallas kernels  64.3 us (90%)
  local copies, waits for them, and re-layouts  5.38 us (8%)
  between operations  0.78 us (1%)
    pallas_call x1, Pallas kernels, per_device(): pl.pallas_call(functools.partial(deposit_kernel, span_y // 2, span_z // 2...  29.1 us
    pallas_call x1, Pallas kernels, per_device(): pl.pallas_call(functools.partial(halo_kernel, counts), out_shape=jax.Shap...  24.2 us
    pallas_call x1, Pallas kernels, per_device(): pl.pallas_call(functools.partial(rows_kernel, counts), out_shape=jax.Shap...  7.86 us
    unnamed x28, local copies, waits for them, and re-layouts  5.3 us
    pallas_call x1, Pallas kernels, per_device(): pl.pallas_call(functools.partial(update_kernel, counts), out_shape=(jax.S...  3.08 us

profile of v1, /device:TPU:0, one launch (start us, length us, event | category | flops | bytes accessed | tf_op | source)
XLA Modules:
  0.0 71.0 jit_solution(13937879874473187728)
XLA Ops:
  0.6 0.0 copy-start.12
  0.6 0.0 copy-start.10
  0.7 0.0 copy-start.8
  0.7 0.0 copy-start
  0.7 1.1 %copy-done = f32[3,512,128]{2,1,0:T(8,128)S(1)} copy-done((f32[3,512,128]{2,1,0:T(8,128)S(1)}, f32[3,512,128]{2,1,0:T(8,128)}, u32[]{:S(2)}) %copy-start) | copy-done | bytes 786456
  1.8 0.0 copy-start.2
  1.8 1.1 %copy-done.2 = f32[3,512,128]{2,1,0:T(8,128)S(1)} copy-done((f32[3,512,128]{2,1,0:T(8,128)S(1)}, f32[3,512,128]{2,1,0:T(8,128)}, u32[]{:S(2)}) %copy-start.2) | copy-done | bytes 786456
  2.9 0.0 copy-start.4
  2.9 0.9 %copy-done.4 = f32[512,128]{1,0:T(8,128)S(1)} copy-done((f32[512,128]{1,0:T(8,128)S(1)}, f32[512,128]{1,0:T(8,128)}, u32[]{:S(2)}) %copy-start.4) | copy-done | bytes 262168
  3.9 0.0 copy-start.7
  3.9 0.7 copy-done.7
  4.6 0.0 copy-start.9
  4.6 0.7 copy-done.9
  5.3 0.0 copy-start.11
  5.3 0.7 copy-done.11
  5.9 0.0 copy-start.1
  5.9 0.0 copy-start.3
  5.9 0.0 copy-start.5
  6.0 7.9 %row_exchange.1 = f32[6,4,8,128]{3,2,1,0:T(8,128)S(1)} custom-call(s32[4,128]{1,0:T(4,128)S(1)} %bitcast.4, s32[512]{0:T(512)S(1)} %copy-done.9, s32[512]{0:T(512)S(1)} %copy-done.11, f32[3,512,128]{2,1,0:T(8,128)S(1)} %copy-done, f32[512,128]{1,0:T(8,128)S(1)} %copy-done.4, f32[3,512,128]{2,1,0:T(8,128)S(1)} %copy-done.2), custom_call_target="tpu_custom_call" | custom-call | tf_op jit(solution)/shard_map/row_exchange/pallas_call | solution.py:355
  13.8 0.5 convert_reduce_fusion
  14.3 0.1 convert_element_type.6.came_ref
  14.4 0.0 copy-done.12
  14.4 0.0 copy-done.10
  14.4 0.0 copy-done.8
  14.4 0.0 copy-done.1
  14.4 0.0 copy-done.3
  14.5 0.0 copy-done.5
  14.5 29.1 %deposit.1.grid_in = f32[12,264,128]{2,1,0:T(8,128)S(1)} custom-call(s32[1]{0:T(128)} %bitcast.me_ref, s32[512]{0:T(512)S(1)} %copy-done.8, s32[512]{0:T(512)S(1)} %copy-done.10, s32[512]{0:T(512)S(1)} %copy-done.12, s32[24]{0:T(128)S(1)} %convert_element_type.6.came_ref, f32[3,512,128]{2,1,0:T(8,128)S(1)} %copy-done.1, f32[512,128]{1,0:T(8,128)S(1)} %copy-done.5, ...), custom_call_target="tpu_custom_call" | custom-call | tf_op jit(solution)/shard_map/deposit/pallas_call | solution.py:373
  43.6 0.0 copy-start.6
  43.6 0.0 copy-start.13
  43.6 24.2 %halo_sums.1.grid_ref = f32[12,264,128]{2,1,0:T(8,128)S(1)} custom-call(f32[12,264,128]{2,1,0:T(8,128)S(1)} %deposit.1.grid_in), custom_call_target="tpu_custom_call" | custom-call | tf_op jit(solution)/shard_map/halo_sums/pallas_call | solution.py:391
  67.9 0.0 copy-done.6
  67.9 0.0 copy-done.13
  67.9 3.1 %grid_update.1 = (f32[8,64,128]{2,1,0:T(8,128)}, f32[3,8,64,128]{3,2,1,0:T(8,128)}) custom-call(f32[12,264,128]{2,1,0:T(8,128)S(1)} %halo_sums.1.grid_ref, s32[8,64,128]{2,1,0:T(8,128)S(1)} %copy-done.6, f32[8]{0:T(128)S(1)} %copy-done.13), custom_call_target="tpu_custom_call" | custom-call | tf_op jit(solution)/shard_map/grid_update/pallas_call | solution.py:411
Async XLA Ops:
  0.6 13.8 %copy-start.12 = (s32[512]{0:T(512)S(1)}, s32[512]{0:T(512)}, u32[]{:S(2)}) copy-start(s32[512]{0:T(512)} %block_ref.3) | copy-start | bytes 6148
  0.6 13.8 %copy-start.10 = (s32[512]{0:T(512)S(1)}, s32[512]{0:T(512)}, u32[]{:S(2)}) copy-start(s32[512]{0:T(512)} %count_ref.3) | copy-start | bytes 6148
  0.7 13.8 %copy-start.8 = (s32[512]{0:T(512)S(1)}, s32[512]{0:T(512)}, u32[]{:S(2)}) copy-start(s32[512]{0:T(512)} %owner_ref.1) | copy-start | bytes 6148
  0.7 1.1 %copy-start = (f32[3,512,128]{2,1,0:T(8,128)S(1)}, f32[3,512,128]{2,1,0:T(8,128)}, u32[]{:S(2)}) copy-start(f32[3,512,128]{2,1,0:T(8,128)} %offs_ref.3) | copy-start | bytes 2359300
  1.8 1.1 %copy-start.2 = (f32[3,512,128]{2,1,0:T(8,128)S(1)}, f32[3,512,128]{2,1,0:T(8,128)}, u32[]{:S(2)}) copy-start(f32[3,512,128]{2,1,0:T(8,128)} %vel_ref.3) | copy-start | bytes 2359300
  2.9 0.9 %copy-start.4 = (f32[512,128]{1,0:T(8,128)S(1)}, f32[512,128]{1,0:T(8,128)}, u32[]{:S(2)}) copy-start(f32[512,128]{1,0:T(8,128)} %mass_ref.3) | copy-start | bytes 786436
  3.9 0.7 copy-start.7
  4.6 0.7 copy-start.9
  5.3 0.7 copy-start.11
  5.9 8.5 %copy-start.1 = (f32[3,512,128]{2,1,0:T(8,128)S(1)}, f32[3,512,128]{2,1,0:T(8,128)}, u32[]{:S(2)}) copy-start(f32[3,512,128]{2,1,0:T(8,128)} %offs_ref.3) | copy-start | bytes 2359300
  5.9 8.5 %copy-start.3 = (f32[3,512,128]{2,1,0:T(8,128)S(1)}, f32[3,512,128]{2,1,0:T(8,128)}, u32[]{:S(2)}) copy-start(f32[3,512,128]{2,1,0:T(8,128)} %vel_ref.3) | copy-start | bytes 2359300
  5.9 8.5 %copy-start.5 = (f32[512,128]{1,0:T(8,128)S(1)}, f32[512,128]{1,0:T(8,128)}, u32[]{:S(2)}) copy-start(f32[512,128]{1,0:T(8,128)} %mass_ref.3) | copy-start | bytes 786436
  43.6 24.3 %copy-start.6 = (s32[8,64,128]{2,1,0:T(8,128)S(1)}, s32[8,64,128]{2,1,0:T(8,128)}, u32[]{:S(2)}) copy-start(s32[8,64,128]{2,1,0:T(8,128)} %mat_ref.1) | copy-start | bytes 786436
  43.6 24.3 %copy-start.13 = (f32[8]{0:T(128)S(1)}, f32[8]{0:T(128)}, u32[]{:S(2)}) copy-start(f32[8]{0:T(128)} %stiff_ref.1) | copy-start | bytes 100

commit v2 on v1

--- a/solution.py
+++ b/solution.py
@@ -42,7 +42,14 @@
                 barrier, inc=1, device_id={axis: target}, device_id_type=pl.DeviceIdType.MESH
             )
         total = total + there.astype(jnp.int32)
-    pl.semaphore_wait(barrier, total)
+    return lambda: pl.semaphore_wait(barrier, total)
+
+
+def load(sources, targets, sems):
+    copies = [pltpu.make_async_copy(s, t, sems.at[n]) for n, (s, t) in enumerate(zip(sources, targets))]
+    for copy in copies:
+        copy.start()
+    return copies
 
 
 def remote(source, target_ref, send_sem, recv_sem, axis, target):
@@ -57,19 +64,29 @@
 
 
 def rows_kernel(
-    counts, owner_ref, count_ref, block_ref, offs_ref, mass_ref, vel_ref, box_ref, out_box, send_sem, recv_sem
+    counts, owner_in, count_in, block_in, offs_in, mass_in, vel_in, box_ref,
+    owner_ref, count_ref, block_ref, offs_ref, mass_ref, vel_ref, out_box, load_sem, send_sem, recv_sem,
 ):
+    loads = load(
+        (owner_in, count_in, block_in, offs_in, mass_in, vel_in),
+        (owner_ref, count_ref, block_ref, offs_ref, mass_ref, vel_ref),
+        load_sem,
+    )
     rows = mass_ref.shape[0]
     size_y, size_z = counts["gy"], counts["gz"]
     myself = (lax.axis_index("gx") * size_y + lax.axis_index("gy")) * size_z + lax.axis_index("gz")
     sides = neighbours(counts)
     box_ref[...] = jnp.zeros_like(box_ref)
+    greeted = greet(sides)
+    loads[0].wait()
     heading = owner_ref[...] - myself
     shape = heading.shape
     place = lax.broadcasted_iota(jnp.int32, shape, 0) * LANES + lax.broadcasted_iota(jnp.int32, shape, 1)
     lane = lax.broadcasted_iota(jnp.int32, (1, LANES), 1)
     steps = (-size_y * size_z, size_y * size_z, -size_z, size_z, -1, 1)
     left = [jnp.where(heading == step, place, rows) for step in steps]
+    for copy in loads[1:]:
+        copy.wait()
     for slot in range(CAP):
         for way in range(6):
             first = jnp.min(left[way])
@@ -83,7 +100,7 @@
             out_box[way, slot, pl.ds(3, 1), :] = jnp.where(lane < live, mass_ref[pl.ds(row, 1), :], 0.0)
             block = jnp.where(valid, block_ref[row], 0).astype(jnp.float32)
             out_box[way, slot, pl.ds(7, 1), :] = jnp.full((1, LANES), block, jnp.float32)
-    greet(sides)
+    greeted()
     copies = [
         remote(out_box.at[way], box_ref.at[way], send_sem.at[way], recv_sem.at[way], axis, target)
         for way, (axis, target, _, _) in enumerate(sides)
@@ -96,11 +113,19 @@
 
 
 def deposit_kernel(
-    half_y, half_z, planes, me_ref, owner_ref, count_ref, block_ref, came_ref,
-    offs_ref, mass_ref, vel_ref, box_ref, out_ref, grid_ref, wx_ref, yk_ref, wz_ref,
+    half_y, half_z, planes, me_ref, came_ref, owner_in, count_in, block_in, offs_in, mass_in, vel_in,
+    box_ref, out_ref, owner_ref, count_ref, block_ref, offs_ref, mass_ref, vel_ref, load_sem,
+    grid_ref, wx_ref, yk_ref, wz_ref, even_ref, odd_ref,
 ):
+    loads = load(
+        (owner_in, count_in, block_in, offs_in, mass_in, vel_in),
+        (owner_ref, count_ref, block_ref.at[pl.ds(0, mass_ref.shape[0])], offs_ref, mass_ref, vel_ref),
+        load_sem,
+    )
     rows = mass_ref.shape[0]
     came = box_ref.shape[0]
+    total = block_ref.shape[0]
+    row_half = even_ref.shape[0]
     sub = lax.broadcasted_iota(jnp.int32, (8, LANES), 0)
     lane = lax.broadcasted_iota(jnp.int32, (8, LANES), 1)
     myself = me_ref[0]
@@ -111,6 +136,8 @@
         return carry
 
     lax.fori_loop(0, grid_ref.shape[0], clear, 0)
+    for copy in loads:
+        copy.wait()
 
     def fill(base, ox, oy, oz, carried):
         for a in range(4):
@@ -138,6 +165,10 @@
         part = [box_ref[pl.ds(group * 64 + c, 8, stride=8), :] for c in range(8)]
         carried = [part[3]] + [part[3] * part[4 + j] for j in range(3)]
         fill(rows + group * 8, part[0], part[1], part[2], carried)
+    for group in range(rows + came // 8, total, 8):
+        fill(group, zero8, zero8, zero8, [zero8] * 4)
+    for row in range(rows, total):
+        block_ref[row] = came_ref[row - rows] if row < rows + came // 8 else 0
 
     def stencil(row):
         parts = []
@@ -168,21 +199,25 @@
             spot = layer + base_x + a
             grid_ref[spot, at, :] = grid_ref[spot, at, :] + sums[a * 16 : a * 16 + 16]
 
+    half = row_half
+    even_ref[...] = jnp.zeros(even_ref.shape, jnp.float32)
+    odd_ref[...] = jnp.zeros(odd_ref.shape, jnp.float32)
+
     def row_group(i, carry):
-        results = [stencil(i * 8 + s) for s in range(8)]
-        for s in range(8):
-            place(block_ref[i * 8 + s], results[s])
-        return carry
-
-    lax.fori_loop(0, rows // 8, row_group, 0)
-
-    def came_group(i, carry):
-        results = [stencil(rows + i * 8 + s) for s in range(8)]
-        for s in range(8):
-            place(came_ref[i * 8 + s], results[s])
-        return carry
-
-    lax.fori_loop(0, came // 64, came_group, 0)
+        base = i * 2 * half
+        for s in range(half):
+            even_ref[s] = stencil(base + s)
+        for s in range(half):
+            place(block_ref[jnp.maximum(base - half + s, 0)], odd_ref[s])
+        for s in range(half):
+            odd_ref[s] = stencil(base + half + s)
+        for s in range(half):
+            place(block_ref[base + s], even_ref[s])
+        return carry
+
+    lax.fori_loop(0, total // (2 * half), row_group, 0)
+    for s in range(half):
+        place(block_ref[total - half + s], odd_ref[s])
 
     def finish(i, carry):
         at = pl.ds(pl.multiple_of(i * 8, 8), 8)
@@ -203,86 +238,130 @@
     lax.fori_loop(0, out_ref.shape[1] // 8, finish, 0)
 
 
-def halo_kernel(counts, grid_in, out_ref, z_box, y_box, x_box, edge_ref, edge_box, send_sem, recv_sem):
+def halo_kernel(
+    counts, grid_in, out_ref, z_box, y_box, x_box, c_box, edge_ref, e_out, e_box, col_ref, send_sem, recv_sem
+):
     planes = out_ref.shape[0] - 2
     tall = out_ref.shape[1]
+    chunks = tall // 8
+    blocks = edge_ref.shape[0] // LANES
     sides = neighbours(counts)
     lane = lax.broadcasted_iota(jnp.int32, (8, LANES), 1)
-    z_box[...] = jnp.zeros_like(z_box)
-    y_box[...] = jnp.zeros_like(y_box)
-    x_box[...] = jnp.zeros_like(x_box)
-    edge_box[...] = jnp.zeros_like(edge_box)
-    greet(sides)
-
-    def exchange(ways, sources, targets, sems):
-        copies = []
-        for way, source, target_ref, sem in zip(ways, sources, targets, sems):
-            axis, target, there, other = sides[way]
-            copy = remote(source, target_ref, send_sem.at[sem], recv_sem.at[sem], axis, target)
-            pl.when(there)(copy.start)
-            copies.append((copy, there, other))
+    for box in (z_box, y_box, x_box, c_box, e_box):
+        box[...] = jnp.zeros_like(box)
+    greet(sides)()
+    first, last = pl.ds(0, 8), pl.ds(tall - 8, 8)
+
+    def begin(way, source, target_ref, sem):
+        axis, target, there, other = sides[way]
+        copy = remote(source, target_ref, send_sem.at[sem], recv_sem.at[sem], axis, target)
+        pl.when(there)(copy.start)
+        return copy, there, other
+
+    def end(copies):
         for copy, there, other in copies:
             pl.when(there)(copy.wait_send)
             pl.when(other)(copy.wait_recv)
 
-    exchange((4, 5), (grid_in.at[planes], grid_in.at[planes + 1]), (z_box.at[0], z_box.at[1]), (4, 5))
+    def roll(value, shift):
+        shift = shift % LANES
+        return pltpu.roll(value, shift, 1) if shift else value
+
+    bulk = [
+        begin(0, grid_in.at[pl.ds(0, 2)], x_box.at[0], 0),
+        begin(1, grid_in.at[pl.ds(planes - 2, 2)], x_box.at[1], 1),
+    ]
+    end([
+        begin(4, grid_in.at[planes], z_box.at[0], 4),
+        begin(5, grid_in.at[planes + 1], z_box.at[1], 5),
+    ])
 
     def add_z(i, carry):
-        at = pl.ds(pl.multiple_of(i * 8, 8), 8)
+        at = pl.ds(i * 8 if isinstance(i, int) else pl.multiple_of(i * 8, 8), 8)
         above, below = z_box[0, at, :], z_box[1, at, :]
         for x in range(planes):
             main = grid_in[x, at, :]
-            main = main + jnp.where(lane == LANES - 1, pltpu.roll(above, LANES - 1 - x, 1), 0.0)
-            down = pltpu.roll(below, LANES - x, 1) if x else below
-            out_ref[x, at, :] = main + jnp.where(lane == 0, down, 0.0)
-        out_ref[planes, at, :] = grid_in[planes, at, :] + pltpu.roll(below, LANES - 16, 1)
-        out_ref[planes + 1, at, :] = grid_in[planes + 1, at, :] + pltpu.roll(above, LANES - 16, 1)
-        return carry
-
-    lax.fori_loop(0, tall // 8, add_z, 0)
-    first, last = pl.ds(0, 8), pl.ds(tall - 8, 8)
-    exchange(
-        (2, 3),
-        (out_ref.at[:, first, :], out_ref.at[:, last, :]),
-        (y_box.at[0], y_box.at[1]),
-        (2, 3),
-    )
+            main = main + jnp.where(lane == LANES - 1, roll(above, LANES - 1 - x), 0.0)
+            out_ref[x, at, :] = main + jnp.where(lane == 0, roll(below, -x), 0.0)
+        out_ref[planes, at, :] = grid_in[planes, at, :] + roll(below, -16)
+        out_ref[planes + 1, at, :] = grid_in[planes + 1, at, :] + roll(above, -16)
+        return carry
+
+    add_z(0, 0)
+    add_z(chunks - 1, 0)
+    across = [
+        begin(2, out_ref.at[:, first, :], y_box.at[0], 2),
+        begin(3, out_ref.at[:, last, :], y_box.at[1], 3),
+    ]
+    lax.fori_loop(1, chunks - 1, add_z, 0)
+    end(across)
+    corner = [
+        begin(0, y_box.at[:, pl.ds(0, 2)], c_box.at[0], 6),
+        begin(1, y_box.at[:, pl.ds(planes - 2, 2)], c_box.at[1], 7),
+    ]
     for x in range(planes + 2):
         out_ref[x, last, :] = out_ref[x, last, :] + y_box[0, x]
         out_ref[x, first, :] = out_ref[x, first, :] + y_box[1, x]
 
     def pack(i, carry):
         at = pl.ds(pl.multiple_of(i * 8, 8), 8)
-        edge_ref[at, :] = jnp.where(lane < 16, out_ref[planes, at, :], pltpu.roll(out_ref[planes + 1, at, :], 16, 1))
-        return carry
-
-    lax.fori_loop(0, tall // 8, pack, 0)
-    exchange(
-        (0, 1, 0, 1),
-        (out_ref.at[pl.ds(0, 2)], out_ref.at[pl.ds(planes - 2, 2)], edge_ref, edge_ref),
-        (x_box.at[0], x_box.at[1], edge_box.at[0], edge_box.at[1]),
-        (0, 1, 6, 7),
-    )
+        zlow, zhigh = out_ref[planes, at, :], out_ref[planes + 1, at, :]
+        above, below = z_box[0, at, :], z_box[1, at, :]
+        value = jnp.where(lane == 0, zlow, jnp.where(lane == 1, roll(zhigh, 1), 0.0))
+        value = jnp.where(lane == 8, roll(zlow, 8 - (planes - 1)), value)
+        value = jnp.where(lane == 9, roll(zhigh, 9 - (planes - 1)), value)
+        value = jnp.where((lane == 2) | (lane == 3), roll(above, 2), value)
+        value = jnp.where((lane == 4) | (lane == 5), roll(below, 4), value)
+        value = jnp.where((lane == 10) | (lane == 11), roll(above, 10 - (planes - 2)), value)
+        value = jnp.where((lane == 12) | (lane == 13), roll(below, 12 - (planes - 2)), value)
+        edge_ref[at, :] = value
+        return carry
+
+    lax.fori_loop(0, chunks, pack, 0)
+    edge_ref[pl.ds(tall, blocks * LANES - tall), :] = jnp.zeros((blocks * LANES - tall, LANES), jnp.float32)
+    for block in range(blocks):
+        at = pl.ds(block * LANES, LANES)
+        turned = jnp.transpose(edge_ref[at, :])
+        e_out[0, :, at] = turned[0:8]
+        e_out[1, :, at] = turned[8:16]
+    corner = corner + [begin(0, e_out.at[0], e_box.at[0], 8), begin(1, e_out.at[1], e_box.at[1], 9)]
+    end(bulk)
+    end(corner)
+    for block in range(blocks):
+        at = pl.ds(block * LANES, LANES)
+        both = jnp.concatenate(
+            [e_box[0, :, at], e_box[1, :, at], jnp.zeros((LANES - 16, LANES), jnp.float32)], 0
+        )
+        col_ref[at, :] = jnp.transpose(both)
+    for p in range(2):
+        high, low = planes - 2 + p, p
+        out_ref[high, last, :] = out_ref[high, last, :] + c_box[0, 0, p]
+        out_ref[high, first, :] = out_ref[high, first, :] + c_box[0, 1, p]
+        out_ref[low, last, :] = out_ref[low, last, :] + c_box[1, 0, p]
+        out_ref[low, first, :] = out_ref[low, first, :] + c_box[1, 1, p]
 
     def add_x(i, carry):
         at = pl.ds(pl.multiple_of(i * 8, 8), 8)
+        col = col_ref[at, :]
+
+        def put(spot, source):
+            return jnp.where(lane == spot, roll(col, spot - source), 0.0)
+
         for p in range(2):
-            out_ref[planes - 2 + p, at, :] = out_ref[planes - 2 + p, at, :] + x_box[0, p, at, :]
-            out_ref[p, at, :] = out_ref[p, at, :] + x_box[1, p, at, :]
-        above, below = edge_box[0, at, :], edge_box[1, at, :]
+            high, low = planes - 2 + p, p
+            out_ref[high, at, :] = (
+                out_ref[high, at, :] + x_box[0, p, at, :] + put(LANES - 1, 2 + p) + put(0, 4 + p)
+            )
+            out_ref[low, at, :] = (
+                out_ref[low, at, :] + x_box[1, p, at, :] + put(LANES - 1, 10 + p) + put(0, 12 + p)
+            )
         for side in range(2):
-            value = out_ref[planes + side, at, :]
-            start = 16 * side
-            value = value + jnp.where(
-                lane == planes - 2, pltpu.roll(above, (planes - 2 - start) % LANES, 1), 0.0
+            out_ref[planes + side, at, :] = (
+                out_ref[planes + side, at, :] + put(planes - 2, side) + put(1, 8 + side)
             )
-            value = value + jnp.where(
-                lane == 1, pltpu.roll(below, (1 - (planes - 1) - start) % LANES, 1), 0.0
-            )
-            out_ref[planes + side, at, :] = value
-        return carry
-
-    lax.fori_loop(0, tall // 8, add_x, 0)
+        return carry
+
+    lax.fori_loop(0, chunks, add_x, 0)
 
 
 def update_kernel(counts, grid_ref, mat_ref, stiff_ref, mass_ref, vel_ref, v_ref, z_ref):
@@ -347,18 +426,27 @@
     span_x, span_y, span_z = material.shape
     planes = span_x + 2
     tall = (span_y + 2) * 4
+    wide = pl.cdiv(tall, LANES) * LANES
     f32 = jnp.float32
     vmem = pl.BlockSpec(memory_space=pltpu.VMEM)
+    hbm = pl.BlockSpec(memory_space=pl.ANY)
     smem = pl.BlockSpec(memory_space=pltpu.SMEM)
     myself = (lax.axis_index("gx") * counts["gy"] + lax.axis_index("gy")) * counts["gz"] + lax.axis_index("gz")
 
     box = pl.pallas_call(
         functools.partial(rows_kernel, counts),
         out_shape=jax.ShapeDtypeStruct((6, CAP, 8, LANES), f32),
-        in_specs=[vmem, smem, smem, vmem, vmem, vmem],
+        in_specs=[hbm] * 6,
         out_specs=vmem,
         scratch_shapes=[
+            pltpu.VMEM((rows // LANES, LANES), jnp.int32),
+            pltpu.SMEM((rows,), jnp.int32),
+            pltpu.SMEM((rows,), jnp.int32),
+            pltpu.VMEM(offsets.shape, f32),
+            pltpu.VMEM(particle_mass.shape, f32),
+            pltpu.VMEM(particle_velocity.shape, f32),
             pltpu.VMEM((6, CAP, 8, LANES), f32),
+            pltpu.SemaphoreType.DMA((6,)),
             pltpu.SemaphoreType.DMA((6,)),
             pltpu.SemaphoreType.DMA((6,)),
         ],
@@ -369,22 +457,32 @@
     )(row_owner.reshape(-1, LANES), row_count, row_block, offsets, particle_mass, particle_velocity)
 
     came_blocks = box[:, :, 7, 0].reshape(-1).astype(jnp.int32)
-    total = rows + 6 * CAP
+    half = 8
+    total = pl.cdiv(rows + 6 * CAP, 2 * half) * 2 * half
     grid = pl.pallas_call(
         functools.partial(deposit_kernel, span_y // 2, span_z // 2, planes),
         out_shape=jax.ShapeDtypeStruct((planes + 2, tall, LANES), f32),
-        in_specs=[smem] * 5 + [vmem] * 4,
+        in_specs=[smem] * 2 + [hbm] * 6 + [vmem],
         out_specs=vmem,
         scratch_shapes=[
+            pltpu.SMEM((rows,), jnp.int32),
+            pltpu.SMEM((rows,), jnp.int32),
+            pltpu.SMEM((total,), jnp.int32),
+            pltpu.VMEM(offsets.shape, f32),
+            pltpu.VMEM(particle_mass.shape, f32),
+            pltpu.VMEM(particle_velocity.shape, f32),
+            pltpu.SemaphoreType.DMA((6,)),
             pltpu.VMEM((3 * planes, tall, LANES), f32),
             pltpu.VMEM((total * 4, LANES), f32),
             pltpu.VMEM((total * 16, LANES), f32),
             pltpu.VMEM((total * 8, LANES), f32),
+            pltpu.VMEM((half, 64, LANES), f32),
+            pltpu.VMEM((half, 64, LANES), f32),
         ],
         compiler_params=pltpu.CompilerParams(vmem_limit_bytes=VMEM_LIMIT),
         name="deposit",
     )(
-        myself.reshape(1), row_owner, row_count, row_block, came_blocks,
+        myself.reshape(1), came_blocks, row_owner, row_count, row_block,
         offsets, particle_mass, particle_velocity, box.reshape(6 * CAP * 8, LANES),
     )
 
@@ -397,10 +495,13 @@
             pltpu.VMEM((2, tall, LANES), f32),
             pltpu.VMEM((2, planes + 2, 8, LANES), f32),
             pltpu.VMEM((2, 2, tall, LANES), f32),
-            pltpu.VMEM((tall, LANES), f32),
-            pltpu.VMEM((2, tall, LANES), f32),
-            pltpu.SemaphoreType.DMA((8,)),
-            pltpu.SemaphoreType.DMA((8,)),
+            pltpu.VMEM((2, 2, 2, 8, LANES), f32),
+            pltpu.VMEM((wide, LANES), f32),
+            pltpu.VMEM((2, 8, wide), f32),
+            pltpu.VMEM((2, 8, wide), f32),
+            pltpu.VMEM((wide, LANES), f32),
+            pltpu.SemaphoreType.DMA((10,)),
+            pltpu.SemaphoreType.DMA((10,)),
         ],
         compiler_params=pltpu.CompilerParams(
             collective_id=1, has_side_effects=True, vmem_limit_bytes=VMEM_LIMIT

time: 71.3 us -> 51.8 us (0.73)
  Pallas kernels: 64.3 us -> 44.9 us
    pallas_call x1, Pallas kernels: 24.2 us -> 15.1 us  [per_device(): pl.pallas_call(functools.partial(halo_kernel, counts), out_shape=jax.Shap...]
    pallas_call x1, Pallas kernels: 29.1 us -> 20.1 us  [per_device(): pl.pallas_call(functools.partial(deposit_kernel, span_y // 2, span_z // 2...]
    pallas_call x1, Pallas kernels: 7.86 us -> 6.63 us  [per_device(): pl.pallas_call(functools.partial(rows_kernel, counts), out_shape=jax.Shap...]
where the time goes in v2:
time: 51.8 us; the launch traced here: 51.5 us
  Pallas kernels  44.9 us (87%)
  local copies, waits for them, and re-layouts  5.38 us (10%)
  between operations  0.78 us (2%)
    pallas_call x1, Pallas kernels, per_device(): pl.pallas_call(functools.partial(deposit_kernel, span_y // 2, span_z // 2...  20.1 us
    pallas_call x1, Pallas kernels, per_device(): pl.pallas_call(functools.partial(halo_kernel, counts), out_shape=jax.Shap...  15.1 us
    pallas_call x1, Pallas kernels, per_device(): pl.pallas_call(functools.partial(rows_kernel, counts), out_shape=jax.Shap...  6.63 us
    unnamed x28, local copies, waits for them, and re-layouts  5.3 us
    pallas_call x1, Pallas kernels, per_device(): pl.pallas_call(functools.partial(update_kernel, counts), out_shape=(jax.S...  3.08 us

profile of v2, /device:TPU:0, one launch (start us, length us, event | category | flops | bytes accessed | tf_op | source)
XLA Modules:
  0.0 51.5 jit_solution(13638636563873680833)
XLA Ops:
  0.6 0.0 copy-start.12
  0.6 0.0 copy-start.10
  0.7 0.0 copy-start.8
  0.7 0.0 copy-start
  0.7 1.1 %copy-done = f32[3,512,128]{2,1,0:T(8,128)S(1)} copy-done((f32[3,512,128]{2,1,0:T(8,128)S(1)}, f32[3,512,128]{2,1,0:T(8,128)}, u32[]{:S(2)}) %copy-start) | copy-done | bytes 786456
  1.8 0.0 copy-start.2
  1.8 1.1 %copy-done.2 = f32[3,512,128]{2,1,0:T(8,128)S(1)} copy-done((f32[3,512,128]{2,1,0:T(8,128)S(1)}, f32[3,512,128]{2,1,0:T(8,128)}, u32[]{:S(2)}) %copy-start.2) | copy-done | bytes 786456
  2.9 0.0 copy-start.4
  2.9 0.9 %copy-done.4 = f32[512,128]{1,0:T(8,128)S(1)} copy-done((f32[512,128]{1,0:T(8,128)S(1)}, f32[512,128]{1,0:T(8,128)}, u32[]{:S(2)}) %copy-start.4) | copy-done | bytes 262168
  3.9 0.0 copy-start.7
  3.9 0.7 %copy-done.7 = s32[512]{0:T(512)S(1)} copy-done((s32[512]{0:T(512)S(1)}, s32[512]{0:T(512)}, u32[]{:S(2)}) %copy-start.7) | copy-done | bytes 2072
  4.6 0.0 copy-start.9
  4.6 0.7 %copy-done.9 = s32[512]{0:T(512)S(1)} copy-done((s32[512]{0:T(512)S(1)}, s32[512]{0:T(512)}, u32[]{:S(2)}) %copy-start.9) | copy-done | bytes 2072
  5.3 0.0 copy-start.11
  5.3 0.7 %copy-done.11 = s32[512]{0:T(512)S(1)} copy-done((s32[512]{0:T(512)S(1)}, s32[512]{0:T(512)}, u32[]{:S(2)}) %copy-start.11) | copy-done | bytes 2072
  5.9 0.0 copy-start.1
  5.9 0.0 copy-start.3
  5.9 0.0 copy-start.5
  6.0 6.6 %row_exchange.1 = f32[6,4,8,128]{3,2,1,0:T(8,128)S(1)} custom-call(s32[4,128]{1,0:T(4,128)S(1)} %bitcast.4, s32[512]{0:T(512)S(1)} %copy-done.9, s32[512]{0:T(512)S(1)} %copy-done.11, f32[3,512,128]{2,1,0:T(8,128)S(1)} %copy-done, f32[512,128]{1,0:T(8,128)S(1)} %copy-done.4, f32[3,512,128]{2,1,0:T(8,128)S(1)} %copy-done.2), custom_call_target="tpu_custom_call" | custom-call | tf_op jit(solution)/shard_map/row_exchange/pallas_call | solution.py:436
  12.6 0.5 convert_reduce_fusion
  13.1 0.1 convert_element_type.6.came_ref
  13.2 0.0 copy-done.12
  13.2 0.0 copy-done.10
  13.2 0.0 copy-done.8
  13.2 0.0 copy-done.1
  13.2 0.0 copy-done.3
  13.2 0.0 copy-done.5
  13.2 20.1 %deposit.1.grid_in = f32[12,264,128]{2,1,0:T(8,128)S(1)} custom-call(s32[1]{0:T(128)} %bitcast.me_ref, s32[24]{0:T(128)S(1)} %convert_element_type.6.came_ref, s32[512]{0:T(512)S(1)} %copy-done.8, s32[512]{0:T(512)S(1)} %copy-done.10, s32[512]{0:T(512)S(1)} %copy-done.12, f32[3,512,128]{2,1,0:T(8,128)S(1)} %copy-done.1, f32[512,128]{1,0:T(8,128)S(1)} %copy-done.5, ...), custom_call_target="tpu_custom_call" | custom-call | tf_op jit(solution)/shard_map/deposit/pallas_call | solution.py:462
  33.3 0.0 copy-start.6
  33.3 0.0 copy-start.13
  33.4 15.1 %halo_sums.1.grid_ref = f32[12,264,128]{2,1,0:T(8,128)S(1)} custom-call(f32[12,264,128]{2,1,0:T(8,128)S(1)} %deposit.1.grid_in), custom_call_target="tpu_custom_call" | custom-call | tf_op jit(solution)/shard_map/halo_sums/pallas_call | solution.py:489
  48.4 0.0 copy-done.6
  48.5 0.0 copy-done.13
  48.5 3.1 %grid_update.1 = (f32[8,64,128]{2,1,0:T(8,128)}, f32[3,8,64,128]{3,2,1,0:T(8,128)}) custom-call(f32[12,264,128]{2,1,0:T(8,128)S(1)} %halo_sums.1.grid_ref, s32[8,64,128]{2,1,0:T(8,128)S(1)} %copy-done.6, f32[8]{0:T(128)S(1)} %copy-done.13), custom_call_target="tpu_custom_call" | custom-call | tf_op jit(solution)/shard_map/grid_update/pallas_call | solution.py:512
Async XLA Ops:
  0.6 12.6 %copy-start.12 = (s32[512]{0:T(512)S(1)}, s32[512]{0:T(512)}, u32[]{:S(2)}) copy-start(s32[512]{0:T(512)} %block_in.3) | copy-start | bytes 6148
  0.6 12.5 %copy-start.10 = (s32[512]{0:T(512)S(1)}, s32[512]{0:T(512)}, u32[]{:S(2)}) copy-start(s32[512]{0:T(512)} %count_in.3) | copy-start | bytes 6148
  0.7 12.5 %copy-start.8 = (s32[512]{0:T(512)S(1)}, s32[512]{0:T(512)}, u32[]{:S(2)}) copy-start(s32[512]{0:T(512)} %owner_in.1) | copy-start | bytes 6148
  0.7 1.1 %copy-start = (f32[3,512,128]{2,1,0:T(8,128)S(1)}, f32[3,512,128]{2,1,0:T(8,128)}, u32[]{:S(2)}) copy-start(f32[3,512,128]{2,1,0:T(8,128)} %offs_in.3) | copy-start | bytes 2359300
  1.8 1.1 %copy-start.2 = (f32[3,512,128]{2,1,0:T(8,128)S(1)}, f32[3,512,128]{2,1,0:T(8,128)}, u32[]{:S(2)}) copy-start(f32[3,512,128]{2,1,0:T(8,128)} %vel_in.3) | copy-start | bytes 2359300
  2.9 0.9 %copy-start.4 = (f32[512,128]{1,0:T(8,128)S(1)}, f32[512,128]{1,0:T(8,128)}, u32[]{:S(2)}) copy-start(f32[512,128]{1,0:T(8,128)} %mass_in.3) | copy-start | bytes 786436
  3.9 0.7 %copy-start.7 = (s32[512]{0:T(512)S(1)}, s32[512]{0:T(512)}, u32[]{:S(2)}) copy-start(s32[512]{0:T(512)} %owner_in.1) | copy-start | bytes 6148
  4.6 0.7 %copy-start.9 = (s32[512]{0:T(512)S(1)}, s32[512]{0:T(512)}, u32[]{:S(2)}) copy-start(s32[512]{0:T(512)} %count_in.3) | copy-start | bytes 6148
  5.3 0.7 %copy-start.11 = (s32[512]{0:T(512)S(1)}, s32[512]{0:T(512)}, u32[]{:S(2)}) copy-start(s32[512]{0:T(512)} %block_in.3) | copy-start | bytes 6148
  5.9 7.3 %copy-start.1 = (f32[3,512,128]{2,1,0:T(8,128)S(1)}, f32[3,512,128]{2,1,0:T(8,128)}, u32[]{:S(2)}) copy-start(f32[3,512,128]{2,1,0:T(8,128)} %offs_in.3) | copy-start | bytes 2359300
  5.9 7.3 %copy-start.3 = (f32[3,512,128]{2,1,0:T(8,128)S(1)}, f32[3,512,128]{2,1,0:T(8,128)}, u32[]{:S(2)}) copy-start(f32[3,512,128]{2,1,0:T(8,128)} %vel_in.3) | copy-start | bytes 2359300
  5.9 7.3 %copy-start.5 = (f32[512,128]{1,0:T(8,128)S(1)}, f32[512,128]{1,0:T(8,128)}, u32[]{:S(2)}) copy-start(f32[512,128]{1,0:T(8,128)} %mass_in.3) | copy-start | bytes 786436
  33.3 15.1 %copy-start.6 = (s32[8,64,128]{2,1,0:T(8,128)S(1)}, s32[8,64,128]{2,1,0:T(8,128)}, u32[]{:S(2)}) copy-start(s32[8,64,128]{2,1,0:T(8,128)} %mat_ref.1) | copy-start | bytes 786436
  33.3 15.1 %copy-start.13 = (f32[8]{0:T(128)S(1)}, f32[8]{0:T(128)}, u32[]{:S(2)}) copy-start(f32[8]{0:T(128)} %stiff_ref.1) | copy-start | bytes 100

commit v3 on v2

--- a/solution.py
+++ b/solution.py
@@ -12,6 +12,7 @@
 gravity_step = 0.05
 AXES = ("gx", "gy", "gz")
 VMEM_LIMIT = 48 * 1024 * 1024
+VMEM_WHOLE = 60 * 1024 * 1024
 
 
 def spline(distance):
@@ -451,13 +452,13 @@
             pltpu.SemaphoreType.DMA((6,)),
         ],
         compiler_params=pltpu.CompilerParams(
-            collective_id=0, has_side_effects=True, vmem_limit_bytes=VMEM_LIMIT
+            collective_id=0, has_side_effects=True, vmem_limit_bytes=VMEM_WHOLE
         ),
         name="row_exchange",
     )(row_owner.reshape(-1, LANES), row_count, row_block, offsets, particle_mass, particle_velocity)
 
     came_blocks = box[:, :, 7, 0].reshape(-1).astype(jnp.int32)
-    half = 8
+    half = 16
     total = pl.cdiv(rows + 6 * CAP, 2 * half) * 2 * half
     grid = pl.pallas_call(
         functools.partial(deposit_kernel, span_y // 2, span_z // 2, planes),

time: 51.8 us -> 48 us (0.927)
  local copies, waits for them, and re-layouts: 5.38 us -> 1 us
  other arithmetic: 0.51 us -> 1.4 us
    unnamed x28 -> x18, local copies, waits for them, and re-layouts: 5.3 us -> 0.93 us
    pallas_call x1, Pallas kernels: 20.1 us -> 18.2 us  [per_device(): pl.pallas_call(functools.partial(deposit_kernel, span_y // 2, span_z // 2...]
    pallas_call x1, Pallas kernels: 6.63 us -> 7.97 us  [per_device(): pl.pallas_call(functools.partial(rows_kernel, counts), out_shape=jax.Shap...]
    convert_element_type x1, other arithmetic: 0.51 us -> 1.4 us  [per_device(): came_blocks = box[:, :, 7, 0].reshape(-1).astype(jnp.int32)]
where the time goes in v3:
time: 48 us; the launch traced here: 47.8 us
  Pallas kernels  44.6 us (93%)
  other arithmetic  1.4 us (3%)
  local copies, waits for them, and re-layouts  1 us (2%)
  between operations  0.79 us (2%)
    pallas_call x1, Pallas kernels, per_device(): pl.pallas_call(functools.partial(deposit_kernel, span_y // 2, span_z // 2...  18.2 us
    pallas_call x1, Pallas kernels, per_device(): pl.pallas_call(functools.partial(halo_kernel, counts), out_shape=jax.Shap...  15.4 us
    pallas_call x1, Pallas kernels, per_device(): pl.pallas_call(functools.partial(rows_kernel, counts), out_shape=jax.Shap...  7.97 us
    pallas_call x1, Pallas kernels, per_device(): pl.pallas_call(functools.partial(update_kernel, counts), out_shape=(jax.S...  3.08 us
    convert_element_type x1, other arithmetic, per_device(): came_blocks = box[:, :, 7, 0].reshape(-1).astype(jnp.int32)  1.4 us

profile of v3, /device:TPU:0, one launch (start us, length us, event | category | flops | bytes accessed | tf_op | source)
XLA Modules:
  0.0 47.8 jit_solution(13523481911179750059)
XLA Ops:
  0.6 0.0 copy-start.1
  0.6 0.0 copy-start.2
  0.7 0.0 copy-start
  0.7 0.0 copy-start.7
  0.7 0.0 copy-start.6
  0.7 0.0 copy-start.5
  0.7 8.0 %row_exchange.1 = f32[6,4,8,128]{3,2,1,0:T(8,128)} custom-call(s32[4,128]{1,0:T(4,128)} %bitcast.4, s32[512]{0:T(512)} %count_in.3, s32[512]{0:T(512)} %block_in.3, f32[3,512,128]{2,1,0:T(8,128)} %offs_in.3, f32[512,128]{1,0:T(8,128)} %mass_in.3, f32[3,512,128]{2,1,0:T(8,128)} %vel_in.3), custom_call_target="tpu_custom_call" | custom-call | tf_op jit(solution)/shard_map/row_exchange/pallas_call | solution.py:437
  8.7 1.4 %convert_reduce_fusion = s32[6,4]{1,0:T(8,128)S(1)} fusion(f32[6,4,8,128]{3,2,1,0:T(8,128)} %row_exchange.1), kind=kLoop, calls=%fused_computation | loop fusion | flops 24 | bytes 192 | tf_op jit(solution)/shard_map/convert_element_type | solution.py:460
  10.1 0.1 convert_element_type.6.came_ref
  10.2 0.0 copy-done.1
  10.2 0.0 copy-done.2
  10.2 0.0 copy-done
  10.2 0.0 copy-done.7
  10.2 0.0 copy-done.6
  10.2 0.0 copy-done.5
  10.2 0.0 copy-start.3
  10.2 0.9 %copy-done.3 = f32[6,4,8,128]{3,2,1,0:T(8,128)S(1)} copy-done((f32[6,4,8,128]{3,2,1,0:T(8,128)S(1)}, f32[6,4,8,128]{3,2,1,0:T(8,128)}, u32[]{:S(2)}) %copy-start.3) | copy-done | bytes 98328
  11.1 18.2 %deposit.1.grid_in = f32[12,264,128]{2,1,0:T(8,128)S(1)} custom-call(s32[1]{0:T(128)} %bitcast.me_ref, s32[24]{0:T(128)S(1)} %convert_element_type.6.came_ref, s32[512]{0:T(512)S(1)} %copy-done.5, s32[512]{0:T(512)S(1)} %copy-done.6, s32[512]{0:T(512)S(1)} %copy-done.7, f32[3,512,128]{2,1,0:T(8,128)S(1)} %copy-done, f32[512,128]{1,0:T(8,128)S(1)} %copy-done.2, ...), custom_call_target="tpu_custom_call" | custom-call | tf_op jit(solution)/shard_map/deposit/pallas_call | solution.py:463
  29.3 0.0 copy-start.4
  29.3 0.0 copy-start.8
  29.3 15.4 %halo_sums.1.grid_ref = f32[12,264,128]{2,1,0:T(8,128)S(1)} custom-call(f32[12,264,128]{2,1,0:T(8,128)S(1)} %deposit.1.grid_in), custom_call_target="tpu_custom_call" | custom-call | tf_op jit(solution)/shard_map/halo_sums/pallas_call | solution.py:490
  44.7 0.0 copy-done.4
  44.7 0.0 copy-done.8
  44.7 3.1 %grid_update.1 = (f32[8,64,128]{2,1,0:T(8,128)}, f32[3,8,64,128]{3,2,1,0:T(8,128)}) custom-call(f32[12,264,128]{2,1,0:T(8,128)S(1)} %halo_sums.1.grid_ref, s32[8,64,128]{2,1,0:T(8,128)S(1)} %copy-done.4, f32[8]{0:T(128)S(1)} %copy-done.8), custom_call_target="tpu_custom_call" | custom-call | tf_op jit(solution)/shard_map/grid_update/pallas_call | solution.py:513
Async XLA Ops:
  0.6 9.5 %copy-start.1 = (f32[3,512,128]{2,1,0:T(8,128)S(1)}, f32[3,512,128]{2,1,0:T(8,128)}, u32[]{:S(2)}) copy-start(f32[3,512,128]{2,1,0:T(8,128)} %vel_in.3) | copy-start | bytes 2359300
  0.6 9.5 %copy-start.2 = (f32[512,128]{1,0:T(8,128)S(1)}, f32[512,128]{1,0:T(8,128)}, u32[]{:S(2)}) copy-start(f32[512,128]{1,0:T(8,128)} %mass_in.3) | copy-start | bytes 786436
  0.7 9.5 %copy-start = (f32[3,512,128]{2,1,0:T(8,128)S(1)}, f32[3,512,128]{2,1,0:T(8,128)}, u32[]{:S(2)}) copy-start(f32[3,512,128]{2,1,0:T(8,128)} %offs_in.3) | copy-start | bytes 2359300
  0.7 9.5 %copy-start.7 = (s32[512]{0:T(512)S(1)}, s32[512]{0:T(512)}, u32[]{:S(2)}) copy-start(s32[512]{0:T(512)} %block_in.3) | copy-start | bytes 6148
  0.7 9.5 %copy-start.6 = (s32[512]{0:T(512)S(1)}, s32[512]{0:T(512)}, u32[]{:S(2)}) copy-start(s32[512]{0:T(512)} %count_in.3) | copy-start | bytes 6148
  0.7 9.5 %copy-start.5 = (s32[512]{0:T(512)S(1)}, s32[512]{0:T(512)}, u32[]{:S(2)}) copy-start(s32[512]{0:T(512)} %owner_in.1) | copy-start | bytes 6148
  10.2 0.9 %copy-start.3 = (f32[6,4,8,128]{3,2,1,0:T(8,128)S(1)}, f32[6,4,8,128]{3,2,1,0:T(8,128)}, u32[]{:S(2)}) copy-start(f32[6,4,8,128]{3,2,1,0:T(8,128)} %row_exchange.1) | copy-start | bytes 294916
  29.3 15.4 %copy-start.4 = (s32[8,64,128]{2,1,0:T(8,128)S(1)}, s32[8,64,128]{2,1,0:T(8,128)}, u32[]{:S(2)}) copy-start(s32[8,64,128]{2,1,0:T(8,128)} %mat_ref.1) | copy-start | bytes 786436
  29.3 15.4 %copy-start.8 = (f32[8]{0:T(128)S(1)}, f32[8]{0:T(128)}, u32[]{:S(2)}) copy-start(f32[8]{0:T(128)} %stiff_ref.1) | copy-start | bytes 100

commit v4 on v3

--- a/solution.py
+++ b/solution.py
@@ -65,7 +65,7 @@
 
 
 def rows_kernel(
-    counts, owner_in, count_in, block_in, offs_in, mass_in, vel_in, box_ref,
+    counts, owner_in, count_in, block_in, offs_in, mass_in, vel_in, box_ref, head_ref,
     owner_ref, count_ref, block_ref, offs_ref, mass_ref, vel_ref, out_box, load_sem, send_sem, recv_sem,
 ):
     loads = load(
@@ -111,16 +111,19 @@
     for way, (_, _, there, other) in enumerate(sides):
         pl.when(there)(copies[way].wait_send)
         pl.when(other)(copies[way].wait_recv)
+    for way in range(6):
+        for slot in range(CAP):
+            head_ref[pl.ds(way * CAP + slot, 1), :] = box_ref[way, slot, pl.ds(7, 1), :]
 
 
 def deposit_kernel(
-    half_y, half_z, planes, me_ref, came_ref, owner_in, count_in, block_in, offs_in, mass_in, vel_in,
-    box_ref, out_ref, owner_ref, count_ref, block_ref, offs_ref, mass_ref, vel_ref, load_sem,
+    half_y, half_z, planes, me_ref, came_in, owner_in, count_in, block_in, offs_in, mass_in, vel_in,
+    box_ref, out_ref, owner_ref, count_ref, block_ref, offs_ref, mass_ref, vel_ref, came_ref, load_sem,
     grid_ref, wx_ref, yk_ref, wz_ref, even_ref, odd_ref,
 ):
     loads = load(
-        (owner_in, count_in, block_in, offs_in, mass_in, vel_in),
-        (owner_ref, count_ref, block_ref.at[pl.ds(0, mass_ref.shape[0])], offs_ref, mass_ref, vel_ref),
+        (owner_in, count_in, block_in, offs_in, mass_in, vel_in, came_in),
+        (owner_ref, count_ref, block_ref.at[pl.ds(0, mass_ref.shape[0])], offs_ref, mass_ref, vel_ref, came_ref),
         load_sem,
     )
     rows = mass_ref.shape[0]
@@ -131,6 +134,8 @@
     lane = lax.broadcasted_iota(jnp.int32, (8, LANES), 1)
     myself = me_ref[0]
     zero8 = jnp.zeros((8, LANES), jnp.float32)
+    low_pair = lax.shift_right_logical((lane + LANES - 1) & (LANES - 1), 1)
+    high_pair = lax.shift_right_logical((lane + 1) & (LANES - 1), 1)
 
     def clear(i, carry):
         grid_ref[i] = jnp.zeros(grid_ref.shape[1:], jnp.float32)
@@ -169,7 +174,7 @@
     for group in range(rows + came // 8, total, 8):
         fill(group, zero8, zero8, zero8, [zero8] * 4)
     for row in range(rows, total):
-        block_ref[row] = came_ref[row - rows] if row < rows + came // 8 else 0
+        block_ref[row] = came_ref[row - rows, 0].astype(jnp.int32) if row < rows + came // 8 else 0
 
     def stencil(row):
         parts = []
@@ -228,10 +233,11 @@
             last = grid_ref[2 * planes + x, at, :]
             main = grid_ref[x, at, :] + jnp.where(lane < LANES - 1, first, 0.0) + jnp.where(lane > 0, last, 0.0)
             out_ref[x, at, :] = main
-            low = jnp.where(lane == x, pltpu.roll(first, x + 1, 1), low)
-            low = jnp.where(lane == 16 + x, pltpu.roll(main, 16 + x, 1), low)
-            high = jnp.where(lane == x, pltpu.roll(last, x, 1) if x else last, high)
-            high = jnp.where(lane == 16 + x, pltpu.roll(main, 17 + x, 1), high)
+            below = pltpu.roll(jnp.where(lane == LANES - 1, first, main), 2 * x + 2, 1)
+            above = jnp.where(lane == 0, last, main)
+            above = pltpu.roll(above, 2 * x, 1) if x else above
+            low = jnp.where(low_pair == x, below, low)
+            high = jnp.where(high_pair == x, above, high)
         out_ref[planes, at, :] = low
         out_ref[planes + 1, at, :] = high
         return carry
@@ -242,12 +248,15 @@
 def halo_kernel(
     counts, grid_in, out_ref, z_box, y_box, x_box, c_box, edge_ref, e_out, e_box, col_ref, send_sem, recv_sem
 ):
-    planes = out_ref.shape[0] - 2
+    planes = out_ref.shape[0] - 1
     tall = out_ref.shape[1]
-    chunks = tall // 8
+    chunks = tall // (24 if tall % 24 == 0 else 8)
     blocks = edge_ref.shape[0] // LANES
     sides = neighbours(counts)
-    lane = lax.broadcasted_iota(jnp.int32, (8, LANES), 1)
+    tile = 24 if tall % 24 == 0 else 8
+    lane = lax.broadcasted_iota(jnp.int32, (tile, LANES), 1)
+    odd = (lane & 1) == 1
+    rim = jnp.logical_or(lane == 0, lane == LANES - 1)
     for box in (z_box, y_box, x_box, c_box, e_box):
         box[...] = jnp.zeros_like(box)
     greet(sides)()
@@ -277,15 +286,17 @@
         begin(5, grid_in.at[planes + 1], z_box.at[1], 5),
     ])
 
+    def received(at):
+        return jnp.where(odd, z_box[0, at, :], roll(z_box[1, at, :], 2))
+
     def add_z(i, carry):
-        at = pl.ds(i * 8 if isinstance(i, int) else pl.multiple_of(i * 8, 8), 8)
-        above, below = z_box[0, at, :], z_box[1, at, :]
+        at = pl.ds(i * tile if isinstance(i, int) else pl.multiple_of(i * tile, 8), tile)
+        both = received(at)
         for x in range(planes):
-            main = grid_in[x, at, :]
-            main = main + jnp.where(lane == LANES - 1, roll(above, LANES - 1 - x), 0.0)
-            out_ref[x, at, :] = main + jnp.where(lane == 0, roll(below, -x), 0.0)
-        out_ref[planes, at, :] = grid_in[planes, at, :] + roll(below, -16)
-        out_ref[planes + 1, at, :] = grid_in[planes + 1, at, :] + roll(above, -16)
+            out_ref[x, at, :] = grid_in[x, at, :] + jnp.where(rim, roll(both, LANES - 2 - 2 * x), 0.0)
+        low = grid_in[planes, at, :] + roll(z_box[1, at, :], 2)
+        high = grid_in[planes + 1, at, :] + roll(z_box[0, at, :], -2)
+        out_ref[planes, at, :] = jnp.where(odd, low, high)
         return carry
 
     add_z(0, 0)
@@ -300,21 +311,19 @@
         begin(0, y_box.at[:, pl.ds(0, 2)], c_box.at[0], 6),
         begin(1, y_box.at[:, pl.ds(planes - 2, 2)], c_box.at[1], 7),
     ]
-    for x in range(planes + 2):
+    for x in range(planes + 1):
         out_ref[x, last, :] = out_ref[x, last, :] + y_box[0, x]
         out_ref[x, first, :] = out_ref[x, first, :] + y_box[1, x]
 
     def pack(i, carry):
-        at = pl.ds(pl.multiple_of(i * 8, 8), 8)
-        zlow, zhigh = out_ref[planes, at, :], out_ref[planes + 1, at, :]
-        above, below = z_box[0, at, :], z_box[1, at, :]
-        value = jnp.where(lane == 0, zlow, jnp.where(lane == 1, roll(zhigh, 1), 0.0))
-        value = jnp.where(lane == 8, roll(zlow, 8 - (planes - 1)), value)
-        value = jnp.where(lane == 9, roll(zhigh, 9 - (planes - 1)), value)
-        value = jnp.where((lane == 2) | (lane == 3), roll(above, 2), value)
-        value = jnp.where((lane == 4) | (lane == 5), roll(below, 4), value)
-        value = jnp.where((lane == 10) | (lane == 11), roll(above, 10 - (planes - 2)), value)
-        value = jnp.where((lane == 12) | (lane == 13), roll(below, 12 - (planes - 2)), value)
+        at = pl.ds(pl.multiple_of(i * tile, 8), tile)
+        zone = out_ref[planes, at, :]
+        both = received(at)
+        value = jnp.where(lane < 14, roll(both, 10 - (2 * planes - 3)), 0.0)
+        value = jnp.where(lane < 10, roll(zone, 8 - (2 * planes - 2)), value)
+        value = jnp.where(lane < 8, 0.0, value)
+        value = jnp.where(lane < 6, roll(both, 1), value)
+        value = jnp.where(lane < 2, zone, value)
         edge_ref[at, :] = value
         return carry
 
@@ -342,24 +351,19 @@
         out_ref[low, first, :] = out_ref[low, first, :] + c_box[1, 1, p]
 
     def add_x(i, carry):
-        at = pl.ds(pl.multiple_of(i * 8, 8), 8)
+        at = pl.ds(pl.multiple_of(i * tile, 8), tile)
         col = col_ref[at, :]
 
-        def put(spot, source):
-            return jnp.where(lane == spot, roll(col, spot - source), 0.0)
+        def put(source):
+            return jnp.where(rim, roll(col, LANES - 1 - source), 0.0)
 
         for p in range(2):
             high, low = planes - 2 + p, p
-            out_ref[high, at, :] = (
-                out_ref[high, at, :] + x_box[0, p, at, :] + put(LANES - 1, 2 + p) + put(0, 4 + p)
-            )
-            out_ref[low, at, :] = (
-                out_ref[low, at, :] + x_box[1, p, at, :] + put(LANES - 1, 10 + p) + put(0, 12 + p)
-            )
-        for side in range(2):
-            out_ref[planes + side, at, :] = (
-                out_ref[planes + side, at, :] + put(planes - 2, side) + put(1, 8 + side)
-            )
+            out_ref[high, at, :] = out_ref[high, at, :] + x_box[0, p, at, :] + put(2 + 2 * p)
+            out_ref[low, at, :] = out_ref[low, at, :] + x_box[1, p, at, :] + put(10 + 2 * p)
+        last_pair = jnp.where((lane == 2 * planes - 4) | (lane == 2 * planes - 3), roll(col, 2 * planes - 4), 0.0)
+        first_pair = jnp.where((lane == 2) | (lane == 3), roll(col, -6), 0.0)
+        out_ref[planes, at, :] = out_ref[planes, at, :] + last_pair + first_pair
         return carry
 
     lax.fori_loop(0, chunks, add_x, 0)
@@ -392,9 +396,9 @@
         return carry
 
     lax.fori_loop(0, planes, fill, 0)
-    for side in range(2):
-        for j, value in enumerate(speeds(planes + side, 1, span_y, there[4 + side])):
-            z_ref[side, j] = value
+    scale = jnp.where((lane & 1) == 1, there[4], there[5])
+    for j, value in enumerate(speeds(planes, 1, span_y, scale)):
+        z_ref[j] = value
 
     def update(x, carry):
         mass_ref[x] = grid_ref[x + 1, pl.ds(4, span_y, stride=4), :]
@@ -406,10 +410,9 @@
             value = v_ref[j, x + 1, pl.ds(8, span_y), :]
             beside = v_ref[j, x + 2, pl.ds(8, span_y), :] + v_ref[j, x, pl.ds(8, span_y), :]
             beside = beside + v_ref[j, x + 1, pl.ds(9, span_y), :] + v_ref[j, x + 1, pl.ds(7, span_y), :]
-            after = pltpu.roll(z_ref[1, j], LANES - 2 - x, 1)
-            before = pltpu.roll(z_ref[0, j], LANES - 1 - x, 1)
-            beside = beside + jnp.where(lane == LANES - 1, after, pltpu.roll(value, LANES - 1, 1))
-            beside = beside + jnp.where(lane == 0, before, pltpu.roll(value, 1, 1))
+            outside = pltpu.roll(z_ref[j], LANES - 3 - 2 * x, 1)
+            beside = beside + jnp.where(lane == LANES - 1, outside, pltpu.roll(value, LANES - 1, 1))
+            beside = beside + jnp.where(lane == 0, outside, pltpu.roll(value, 1, 1))
             result = value + stiff * (beside - 6.0 * value)
             if j == 2:
                 result = result - gravity_step
@@ -434,11 +437,14 @@
     smem = pl.BlockSpec(memory_space=pltpu.SMEM)
     myself = (lax.axis_index("gx") * counts["gy"] + lax.axis_index("gy")) * counts["gz"] + lax.axis_index("gz")
 
-    box = pl.pallas_call(
+    box, heads = pl.pallas_call(
         functools.partial(rows_kernel, counts),
-        out_shape=jax.ShapeDtypeStruct((6, CAP, 8, LANES), f32),
+        out_shape=(
+            jax.ShapeDtypeStruct((6, CAP, 8, LANES), f32),
+            jax.ShapeDtypeStruct((6 * CAP, LANES), f32),
+        ),
         in_specs=[hbm] * 6,
-        out_specs=vmem,
+        out_specs=(vmem, vmem),
         scratch_shapes=[
             pltpu.VMEM((rows // LANES, LANES), jnp.int32),
             pltpu.SMEM((rows,), jnp.int32),
@@ -457,13 +463,12 @@
         name="row_exchange",
     )(row_owner.reshape(-1, LANES), row_count, row_block, offsets, particle_mass, particle_velocity)
 
-    came_blocks = box[:, :, 7, 0].reshape(-1).astype(jnp.int32)
     half = 16
     total = pl.cdiv(rows + 6 * CAP, 2 * half) * 2 * half
     grid = pl.pallas_call(
         functools.partial(deposit_kernel, span_y // 2, span_z // 2, planes),
         out_shape=jax.ShapeDtypeStruct((planes + 2, tall, LANES), f32),
-        in_specs=[smem] * 2 + [hbm] * 6 + [vmem],
+        in_specs=[smem] + [hbm] * 7 + [vmem],
         out_specs=vmem,
         scratch_shapes=[
             pltpu.SMEM((rows,), jnp.int32),
@@ -472,7 +477,8 @@
             pltpu.VMEM(offsets.shape, f32),
             pltpu.VMEM(particle_mass.shape, f32),
             pltpu.VMEM(particle_velocity.shape, f32),
-            pltpu.SemaphoreType.DMA((6,)),
+            pltpu.SMEM((6 * CAP, LANES), f32),
+            pltpu.SemaphoreType.DMA((7,)),
             pltpu.VMEM((3 * planes, tall, LANES), f32),
             pltpu.VMEM((total * 4, LANES), f32),
             pltpu.VMEM((total * 16, LANES), f32),
@@ -483,18 +489,18 @@
         compiler_params=pltpu.CompilerParams(vmem_limit_bytes=VMEM_LIMIT),
         name="deposit",
     )(
-        myself.reshape(1), came_blocks, row_owner, row_count, row_block,
+        myself.reshape(1), heads, row_owner, row_count, row_block,
         offsets, particle_mass, particle_velocity, box.reshape(6 * CAP * 8, LANES),
     )
 
     grid = pl.pallas_call(
         functools.partial(halo_kernel, counts),
-        out_shape=jax.ShapeDtypeStruct((planes + 2, tall, LANES), f32),
+        out_shape=jax.ShapeDtypeStruct((planes + 1, tall, LANES), f32),
         in_specs=[vmem],
         out_specs=vmem,
         scratch_shapes=[
             pltpu.VMEM((2, tall, LANES), f32),
-            pltpu.VMEM((2, planes + 2, 8, LANES), f32),
+            pltpu.VMEM((2, planes + 1, 8, LANES), f32),
             pltpu.VMEM((2, 2, tall, LANES), f32),
             pltpu.VMEM((2, 2, 2, 8, LANES), f32),
             pltpu.VMEM((wide, LANES), f32),
@@ -520,7 +526,7 @@
         out_specs=(vmem, vmem),
         scratch_shapes=[
             pltpu.VMEM((3, planes, span_y + 16, LANES), f32),
-            pltpu.VMEM((2, 3, span_y, LANES), f32),
+            pltpu.VMEM((3, span_y, LANES), f32),
         ],
         compiler_params=pltpu.CompilerParams(vmem_limit_bytes=VMEM_LIMIT),
         name="grid_update",

time: 48 us -> 43.5 us (0.906)
  Pallas kernels: 44.6 us -> 40.8 us
  other arithmetic: 1.4 us -> 0 us
  local copies, waits for them, and re-layouts: 1 us -> 1.63 us
    pallas_call x1, Pallas kernels: 15.4 us -> 12.8 us  [per_device(): pl.pallas_call(functools.partial(halo_kernel, counts), out_shape=jax.Shap...]
    convert_element_type x1 -> x0, other arithmetic: 1.4 us -> none  [per_device(): came_blocks = box[:, :, 7, 0].reshape(-1).astype(jnp.int32)]
    pallas_call x1, Pallas kernels: 18.2 us -> 17.3 us  [per_device(): pl.pallas_call(functools.partial(deposit_kernel, span_y // 2, span_z // 2...]
    unnamed x18 -> x20, local copies, waits for them, and re-layouts: 0.93 us -> 1.63 us
where the time goes in v4:
time: 43.5 us; the launch traced here: 43.3 us
  Pallas kernels  40.8 us (94%)
  local copies, waits for them, and re-layouts  1.63 us (4%)
  between operations  0.8 us (2%)
    pallas_call x1, Pallas kernels, per_device(): pl.pallas_call(functools.partial(deposit_kernel, span_y // 2, span_z // 2...  17.3 us
    pallas_call x1, Pallas kernels, per_device(): pl.pallas_call(functools.partial(halo_kernel, counts), out_shape=jax.Shap...  12.8 us
    pallas_call x1, Pallas kernels, per_device(): pl.pallas_call(functools.partial(rows_kernel, counts), out_shape=(jax.Sha...  7.97 us
    pallas_call x1, Pallas kernels, per_device(): pl.pallas_call(functools.partial(update_kernel, counts), out_shape=(jax.S...  2.85 us
    unnamed x20, local copies, waits for them, and re-layouts  1.63 us

profile of v4, /device:TPU:0, one launch (start us, length us, event | category | flops | bytes accessed | tf_op | source)
XLA Modules:
  0.0 43.3 jit_solution(14729784100760430311)
XLA Ops:
  0.6 0.0 copy-start.1
  0.6 0.0 copy-start.2
  0.7 0.0 copy-start
  0.7 0.0 copy-start.8
  0.7 0.0 copy-start.7
  0.7 0.0 copy-start.6
  0.7 8.0 %row_exchange.1 = (f32[6,4,8,128]{3,2,1,0:T(8,128)}, f32[24,128]{1,0:T(8,128)}) custom-call(s32[4,128]{1,0:T(4,128)} %bitcast.4, s32[512]{0:T(512)} %count_in.3, s32[512]{0:T(512)} %block_in.3, f32[3,512,128]{2,1,0:T(8,128)} %offs_in.3, f32[512,128]{1,0:T(8,128)} %mass_in.3, f32[3,512,128]{2,1,0:T(8,128)} %vel_in.3), custom_call_target="tpu_custom_call" | custom-call | tf_op jit(solution)/shard_map/row_exchange/pallas_call | solution.py:440
  8.7 0.0 copy-done.1
  8.7 0.0 copy-done.2
  8.7 0.0 copy-done
  8.7 0.0 copy-done.8
  8.7 0.0 copy-done.7
  8.7 0.0 copy-done.6
  8.7 0.0 copy-start.4
  8.8 0.9 %copy-done.4 = f32[6,4,8,128]{3,2,1,0:T(8,128)S(1)} copy-done((f32[6,4,8,128]{3,2,1,0:T(8,128)S(1)}, f32[6,4,8,128]{3,2,1,0:T(8,128)}, u32[]{:S(2)}) %copy-start.4) | copy-done | bytes 98328
  9.6 0.0 copy-start.5
  9.6 0.7 %copy-done.5 = f32[24,128]{1,0:T(8,128)S(1)} copy-done((f32[24,128]{1,0:T(8,128)S(1)}, f32[24,128]{1,0:T(8,128)}, u32[]{:S(2)}) %copy-start.5) | copy-done | bytes 12312
  10.3 17.3 %deposit.1.grid_in = f32[12,264,128]{2,1,0:T(8,128)S(1)} custom-call(s32[1]{0:T(128)} %bitcast.me_ref, f32[24,128]{1,0:T(8,128)S(1)} %copy-done.5, s32[512]{0:T(512)S(1)} %copy-done.6, s32[512]{0:T(512)S(1)} %copy-done.7, s32[512]{0:T(512)S(1)} %copy-done.8, f32[3,512,128]{2,1,0:T(8,128)S(1)} %copy-done, f32[512,128]{1,0:T(8,128)S(1)} %copy-done.2, ...), custom_call_target="tpu_custom_call" | custom-call | tf_op jit(solution)/shard_map/deposit/pallas_call | solution.py:468
  27.6 0.0 copy-start.3
  27.6 0.0 copy-start.9
  27.6 12.8 %halo_sums.1.grid_ref = f32[11,264,128]{2,1,0:T(8,128)S(1)} custom-call(f32[12,264,128]{2,1,0:T(8,128)S(1)} %deposit.1.grid_in), custom_call_target="tpu_custom_call" | custom-call | tf_op jit(solution)/shard_map/halo_sums/pallas_call | solution.py:496
  40.4 0.0 copy-done.3
  40.4 0.0 copy-done.9
  40.4 2.8 %grid_update.1 = (f32[8,64,128]{2,1,0:T(8,128)}, f32[3,8,64,128]{3,2,1,0:T(8,128)}) custom-call(f32[11,264,128]{2,1,0:T(8,128)S(1)} %halo_sums.1.grid_ref, s32[8,64,128]{2,1,0:T(8,128)S(1)} %copy-done.3, f32[8]{0:T(128)S(1)} %copy-done.9), custom_call_target="tpu_custom_call" | custom-call | tf_op jit(solution)/shard_map/grid_update/pallas_call | solution.py:519
Async XLA Ops:
  0.6 8.1 %copy-start.1 = (f32[3,512,128]{2,1,0:T(8,128)S(1)}, f32[3,512,128]{2,1,0:T(8,128)}, u32[]{:S(2)}) copy-start(f32[3,512,128]{2,1,0:T(8,128)} %vel_in.3) | copy-start | bytes 2359300
  0.6 8.1 %copy-start.2 = (f32[512,128]{1,0:T(8,128)S(1)}, f32[512,128]{1,0:T(8,128)}, u32[]{:S(2)}) copy-start(f32[512,128]{1,0:T(8,128)} %mass_in.3) | copy-start | bytes 786436
  0.7 8.1 %copy-start = (f32[3,512,128]{2,1,0:T(8,128)S(1)}, f32[3,512,128]{2,1,0:T(8,128)}, u32[]{:S(2)}) copy-start(f32[3,512,128]{2,1,0:T(8,128)} %offs_in.3) | copy-start | bytes 2359300
  0.7 8.1 %copy-start.8 = (s32[512]{0:T(512)S(1)}, s32[512]{0:T(512)}, u32[]{:S(2)}) copy-start(s32[512]{0:T(512)} %block_in.3) | copy-start | bytes 6148
  0.7 8.1 %copy-start.7 = (s32[512]{0:T(512)S(1)}, s32[512]{0:T(512)}, u32[]{:S(2)}) copy-start(s32[512]{0:T(512)} %count_in.3) | copy-start | bytes 6148
  0.7 8.1 %copy-start.6 = (s32[512]{0:T(512)S(1)}, s32[512]{0:T(512)}, u32[]{:S(2)}) copy-start(s32[512]{0:T(512)} %owner_in.1) | copy-start | bytes 6148
  8.7 0.9 %copy-start.4 = (f32[6,4,8,128]{3,2,1,0:T(8,128)S(1)}, f32[6,4,8,128]{3,2,1,0:T(8,128)}, u32[]{:S(2)}) copy-start(f32[6,4,8,128]{3,2,1,0:T(8,128)} %get-tuple-element.5) | copy-start | bytes 294916
  9.6 0.7 %copy-start.5 = (f32[24,128]{1,0:T(8,128)S(1)}, f32[24,128]{1,0:T(8,128)}, u32[]{:S(2)}) copy-start(f32[24,128]{1,0:T(8,128)} %get-tuple-element.4.came_in) | copy-start | bytes 36868
  27.6 12.8 %copy-start.3 = (s32[8,64,128]{2,1,0:T(8,128)S(1)}, s32[8,64,128]{2,1,0:T(8,128)}, u32[]{:S(2)}) copy-start(s32[8,64,128]{2,1,0:T(8,128)} %mat_ref.1) | copy-start | bytes 786436
  27.6 12.8 %copy-start.9 = (f32[8]{0:T(128)S(1)}, f32[8]{0:T(128)}, u32[]{:S(2)}) copy-start(f32[8]{0:T(128)} %stiff_ref.1) | copy-start | bytes 100
